TPU v7x, 256 devices: a whole 4x4x8 slice. The times are simulated.
256 devices in a mesh: batch: 64 (over z, y, x_lo), tower: 4 (over x_hi, core).
Axes of the slice: x: 4 (x_hi: 2, x_lo: 2; x = x_hi * 2 + x_lo), y: 4, z: 8, core: 2. Of those that a mesh axis runs over, the one named last changes fastest.
Arguments:
- prompt_feats: bfloat16 [24576, 1152], P('batch', 'tower'), may hold values from -6 to 6
- response_feats: bfloat16 [24576, 1152], P('batch', 'tower'), may hold values from -6 to 6
- prompt_proj: bfloat16 [1152, 1152], P('tower'), may hold values from -0.1875 to 0.1875
- response_proj: bfloat16 [1152, 1152], P('tower'), may hold values from -0.1875 to 0.1875
- logit_scale: float32 [1], replicated, may hold values from 4 to 10
- logit_bias: float32 [1], replicated, may hold values from -2 to 0
- teacher: int32 [24576, 3072], P('batch'), may hold values from -127 to 127
- valid: int32 [24576, 8], P('batch'), may hold values from 0 to 1, as said below
Outputs:
- grad_prompt: bfloat16 [24576, 1152], P('batch', 'tower')
- grad_response: bfloat16 [24576, 1152], P('batch', 'tower')
- loss: float32 [1], replicated
Inputs may be any that keep to these rules, and one draw needn't show every extreme that they name: valid holds only 0 and 1.
All inputs are finite; a program needn't handle non-finite values.
Results may differ from a plain program's by a relative error of at most 0.0065.
Values may be sent and summed in bfloat16 or wider, within the bound.
A program may use at most 128 MiB of HBM per device.

v0:
```python
import jax
import jax.numpy as jnp
from jax import lax
from jax.sharding import PartitionSpec as P


def from_behind(x, axis, by):
    peers = lax.axis_size(axis)
    return lax.ppermute(x, axis, [(i, (i + by) % peers) for i in range(peers)])


def unit_rows(pre):
    norm = jnp.sqrt(jnp.sum(pre * pre, axis=1, keepdims=True) + 1e-06)
    return (pre / norm, norm)


def back_rows(grad, unit, norm):
    inner = jnp.sum(unit * grad, axis=1, keepdims=True)
    return ((grad - unit * inner) / norm).astype(jnp.bfloat16)


def on_device(
    prompt_feats,
    response_feats,
    prompt_proj,
    response_proj,
    logit_scale,
    logit_bias,
    teacher,
    valid,
):
    rows = prompt_feats.shape[0]
    steps = valid.shape[1]
    part_p = jnp.dot(prompt_feats, prompt_proj, preferred_element_type=jnp.float32)
    part_r = jnp.dot(response_feats, response_proj, preferred_element_type=jnp.float32)
    pre_p, pre_r = lax.psum((part_p, part_r), "tower")
    unit_p, norm_p = unit_rows(pre_p)
    unit_r, norm_r = unit_rows(pre_r)
    emb_p = unit_p.astype(jnp.bfloat16)
    emb_r = unit_r.astype(jnp.bfloat16)
    scale = logit_scale[0]
    bias = logit_bias[0]
    current = emb_r
    grad_prom = jnp.zeros((rows, emb_p.shape[1]), jnp.float32)
    grad_home_sum = jnp.zeros((rows, emb_p.shape[1]), jnp.float32)
    carried = grad_home_sum
    loss_sum = jnp.zeros((), jnp.float32)
    for step in range(steps):
        if step > 0:
            current = from_behind(current, "batch", 1)
        score = (
            scale
            * lax.dot_general(
                emb_p, current, (((1,), (1,)), ((), ())), preferred_element_type=jnp.float32
            )
            + bias
        )
        target = jax.nn.sigmoid(
            teacher[:, step * rows : (step + 1) * rows].astype(jnp.float32) / 32.0
        )
        weight = valid[:, step : step + 1].astype(jnp.float32)
        loss_sum = loss_sum + jnp.sum(weight * (jax.nn.softplus(score) - target * score))
        coef = (scale * weight * (jax.nn.sigmoid(score) - target)).astype(jnp.bfloat16)
        grad_prom = grad_prom + jnp.dot(coef, current, preferred_element_type=jnp.float32)
        term = lax.dot_general(
            coef, emb_p, (((0,), (0,)), ((), ())), preferred_element_type=jnp.float32
        )
        if step > 0:
            carried = from_behind(carried, "batch", 1) + term
        else:
            carried = term
    owned_r = from_behind(carried, "batch", -(steps - 1))
    d_p = back_rows(grad_prom, unit_p, norm_p)
    d_r = back_rows(owned_r, unit_r, norm_r)
    grad_prompt = lax.dot_general(
        d_p, prompt_proj, (((1,), (1,)), ((), ())), preferred_element_type=jnp.float32
    ).astype(jnp.bfloat16)
    grad_response = lax.dot_general(
        d_r, response_proj, (((1,), (1,)), ((), ())), preferred_element_type=jnp.float32
    ).astype(jnp.bfloat16)
    total = lax.psum(loss_sum, "batch")
    loss = (total / (rows * lax.axis_size("batch") * steps * rows)).reshape(1)
    return (grad_prompt, grad_response, loss)


def solution(mesh):
    in_specs = (
        P("batch", "tower"),
        P("batch", "tower"),
        P("tower", None),
        P("tower", None),
        P(),
        P(),
        P("batch", None),
        P("batch", None),
    )
    out_specs = (P("batch", "tower"), P("batch", "tower"), P())
    return jax.shard_map(
        on_device, mesh=mesh, in_specs=in_specs, out_specs=out_specs, check_vma=False
    )
```

profile of v0, /device:TPU:4, one launch (start us, length us, event | category | flops | bytes accessed | tf_op | source)
XLA Modules:
  0.0 754.0 jit_solution(17352857350239556776)
XLA Ops:
  8.3 2.8 fusion.40
  11.1 1.9 fusion.41
  14.5 86.1 %all-reduce.3.cloned.1.call-done = (f32[384,1152]{1,0:T(8,128)}, f32[384,1152]{1,0:T(8,128)}) async-done(((f32[384,1152]{1,0:T(8,128)}, f32[384,1152]{1,0:T(8,128)}), (f32[384,1152]{1,0:T(8,128)}, f32[384,1152]{1,0:T(8,128)})) %all-reduce.3.cloned.1.call-update) | async-done | bytes 3538960 | tf_op jit(solution)/shard_map/psum | solution.py:36
  103.0 3.0 collective-permute-start
  106.8 24.1 %collective-permute-done = bf16[384,1152]{1,0:T(8,128)(2,1)S(1)} collective-permute-done((bf16[384,1152]{1,0:T(8,128)(2,1)S(1)}, bf16[384,1152]{1,0:T(8,128)(2,1)S(1)}, u32[]{:S(2)}, u32[]{:S(2)}) %collective-permute-start) | collective-permute-done | bytes 884768 | tf_op jit(solution)/shard_map/ppermute | solution.py:9
  130.9 2.2 fusion.13
  133.9 44.4 %collective-permute-done.7 = f32[384,1152]{1,0:T(8,128)S(1)} collective-permute-done((f32[384,1152]{1,0:T(8,128)S(1)}, f32[384,1152]{1,0:T(8,128)S(1)}, u32[]{:S(2)}, u32[]{:S(2)}) %collective-permute-start.7) | collective-permute-done | bytes 1769504 | tf_op jit(solution)/shard_map/ppermute | solution.py:9
  179.4 62.4 %collective-permute-done.1 = bf16[384,1152]{1,0:T(8,128)(2,1)S(1)} collective-permute-done((bf16[384,1152]{1,0:T(8,128)(2,1)S(1)}, bf16[384,1152]{1,0:T(8,128)(2,1)S(1)}, u32[]{:S(2)}, u32[]{:S(2)}) %collective-permute-start.1) | collective-permute-done | bytes 884768 | tf_op jit(solution)/shard_map/ppermute | solution.py:9
  244.0 61.3 %collective-permute-done.2 = bf16[384,1152]{1,0:T(8,128)(2,1)S(1)} collective-permute-done((bf16[384,1152]{1,0:T(8,128)(2,1)S(1)}, bf16[384,1152]{1,0:T(8,128)(2,1)S(1)}, u32[]{:S(2)}, u32[]{:S(2)}) %collective-permute-start.2) | collective-permute-done | bytes 884768 | tf_op jit(solution)/shard_map/ppermute | solution.py:9
  307.2 60.5 %collective-permute-done.3 = bf16[384,1152]{1,0:T(8,128)(2,1)S(1)} collective-permute-done((bf16[384,1152]{1,0:T(8,128)(2,1)S(1)}, bf16[384,1152]{1,0:T(8,128)(2,1)S(1)}, u32[]{:S(2)}, u32[]{:S(2)}) %collective-permute-start.3) | collective-permute-done | bytes 884768 | tf_op jit(solution)/shard_map/ppermute | solution.py:9
  369.7 59.7 %collective-permute-done.4 = bf16[384,1152]{1,0:T(8,128)(2,1)} collective-permute-done((bf16[384,1152]{1,0:T(8,128)(2,1)S(1)}, bf16[384,1152]{1,0:T(8,128)(2,1)}, u32[]{:S(2)}, u32[]{:S(2)}) %collective-permute-start.4) | collective-permute-done | bytes 884768 | tf_op jit(solution)/shard_map/ppermute | solution.py:9
  433.6 1.9 fusion.42
  436.8 3.1 convolution_add_fusion.7
  439.9 2.0 convolution_add_fusion.6
  441.9 50.8 %collective-permute-done.5 = bf16[384,1152]{1,0:T(8,128)(2,1)} collective-permute-done((bf16[384,1152]{1,0:T(8,128)(2,1)}, bf16[384,1152]{1,0:T(8,128)(2,1)}, u32[]{:S(2)}, u32[]{:S(2)}) %collective-permute-start.5) | collective-permute-done | bytes 884768 | tf_op jit(solution)/shard_map/ppermute | solution.py:9
  499.5 20.2 %collective-permute-done.6 = bf16[384,1152]{1,0:T(8,128)(2,1)S(1)} collective-permute-done((bf16[384,1152]{1,0:T(8,128)(2,1)}, bf16[384,1152]{1,0:T(8,128)(2,1)S(1)}, u32[]{:S(2)}, u32[]{:S(2)}) %collective-permute-start.6) | collective-permute-done | bytes 884768 | tf_op jit(solution)/shard_map/ppermute | solution.py:9
  519.7 4.0 fusion.31
  524.6 38.9 %collective-permute-done.13 = f32[384,1152]{1,0:T(8,128)S(1)} collective-permute-done((f32[384,1152]{1,0:T(8,128)S(1)}, f32[384,1152]{1,0:T(8,128)S(1)}, u32[]{:S(2)}, u32[]{:S(2)}) %collective-permute-start.13) | collective-permute-done | bytes 1769504 | tf_op jit(solution)/shard_map/ppermute | solution.py:9
  564.9 3.3 convolution_add_fusion.3
  571.9 4.3 convolution_add_fusion.2
  576.2 159.5 %psum.23 = f32[]{:T(128)} all-reduce(f32[]{:T(128)S(6)} %add.247), channel_id=1, replica_groups=mesh['batch'=64,'tower'=4] {'batch'}, use_global_device_ids=true, to_apply=%region_14.15 | all-reduce | flops 1 | bytes 8 | tf_op jit(solution)/shard_map/psum | solution.py:81
  736.4 3.5 multiply_reduce_fusion.1
  741.2 1.9 multiply_reduce_fusion
  743.2 2.9 convolution_convert_fusion
  (115 shorter events, 26.6 us)
Async XLA Ops:
  7.2 93.3 %all-reduce.3.cloned.1.call-start = ((), (), s32[]{:S(2)}) async-start(), calls=%async_computation | async-start | bytes 7077888 | tf_op jit(solution)/shard_map/psum | solution.py:36
  103.0 27.9 %collective-permute-start = (bf16[384,1152]{1,0:T(8,128)(2,1)S(1)}, bf16[384,1152]{1,0:T(8,128)(2,1)S(1)}, u32[]{:S(2)}, u32[]{:S(2)}) collective-permute-start(bf16[384,1152]{1,0:T(8,128)(2,1)S(1)} %fusion.33), channel_id=1, source_target_pairs={{0,4},{4,8},{8,12},{12,16},{16,20},{20,24},{24,28},{28,32},{32,36}... | collective-permute-start | bytes 2654216 | tf_op jit(solution)/shard_map/ppermute | solution.py:9
  105.9 25.0 %copy-start.8 = (s32[384,3072]{1,0:T(8,128)S(1)}, s32[384,3072]{1,0:T(8,128)}, u32[]{:S(2)}) copy-start(s32[384,3072]{1,0:T(8,128)} %param.14) | copy-start | bytes 14155780
  130.9 48.4 %copy-start.9 = (bf16[384,1152]{1,0:T(8,128)(2,1)}, bf16[384,1152]{1,0:T(8,128)(2,1)S(1)}, u32[]{:S(2)}) copy-start(bf16[384,1152]{1,0:T(8,128)(2,1)S(1)} %collective-permute-done) | copy-start | bytes 2654212
  133.1 45.2 %copy-start.27 = (f32[384,384]{1,0:T(8,128)}, f32[384,384]{1,0:T(8,128)S(1)}, u32[]{:S(2)}) copy-start(f32[384,384]{1,0:T(8,128)S(1)} %get-tuple-element.30) | copy-start | bytes 1769476
  133.8 44.5 %collective-permute-start.7 = (f32[384,1152]{1,0:T(8,128)S(1)}, f32[384,1152]{1,0:T(8,128)S(1)}, u32[]{:S(2)}, u32[]{:S(2)}) collective-permute-start(f32[384,1152]{1,0:T(8,128)S(1)} %fusion.43), channel_id=1, source_target_pairs={{0,4},{4,8},{8,12},{12,16},{16,20},{20,24},{24,28},{28,32},{32,36}... | collective-permute-start | bytes 5308424 | tf_op jit(solution)/shard_map/ppermute | solution.py:9
  179.2 64.2 %collective-permute-start.8 = (f32[384,1152]{1,0:T(8,128)S(1)}, f32[384,1152]{1,0:T(8,128)S(1)}, u32[]{:S(2)}, u32[]{:S(2)}) collective-permute-start(f32[384,1152]{1,0:T(8,128)S(1)} %convolution_add_fusion), channel_id=1, source_target_pairs={{0,4},{4,8},{8,12},{12,16},{16,20},{20,24},{24,28},{28,32},{32,36}... | collective-permute-start | bytes 5308424 | tf_op jit(solution)/shard_map/ppermute | solution.py:9
  179.3 62.5 %collective-permute-start.1 = (bf16[384,1152]{1,0:T(8,128)(2,1)S(1)}, bf16[384,1152]{1,0:T(8,128)(2,1)S(1)}, u32[]{:S(2)}, u32[]{:S(2)}) collective-permute-start(bf16[384,1152]{1,0:T(8,128)(2,1)S(1)} %collective-permute-done), channel_id=1, source_target_pairs={{0,4},{4,8},{8,12},{12,16},{16,20},{20,24},{24,28},{28,32},{32,36}... | collective-permute-start | bytes 2654216 | tf_op jit(solution)/shard_map/ppermute | solution.py:9
  243.6 63.2 %collective-permute-start.9 = (f32[384,1152]{1,0:T(8,128)S(1)}, f32[384,1152]{1,0:T(8,128)S(1)}, u32[]{:S(2)}, u32[]{:S(2)}) collective-permute-start(f32[384,1152]{1,0:T(8,128)S(1)} %add.227), channel_id=1, source_target_pairs={{0,4},{4,8},{8,12},{12,16},{16,20},{20,24},{24,28},{28,32},{32,36}... | collective-permute-start | bytes 5308424 | tf_op jit(solution)/shard_map/ppermute | solution.py:9
  243.7 61.6 %collective-permute-start.2 = (bf16[384,1152]{1,0:T(8,128)(2,1)S(1)}, bf16[384,1152]{1,0:T(8,128)(2,1)S(1)}, u32[]{:S(2)}, u32[]{:S(2)}) collective-permute-start(bf16[384,1152]{1,0:T(8,128)(2,1)S(1)} %collective-permute-done.1), channel_id=1, source_target_pairs={{0,4},{4,8},{8,12},{12,16},{16,20},{20,24},{24,28},{28,32},{32,36}... | collective-permute-start | bytes 2654216 | tf_op jit(solution)/shard_map/ppermute | solution.py:9
  307.0 62.3 %collective-permute-start.10 = (f32[384,1152]{1,0:T(8,128)S(1)}, f32[384,1152]{1,0:T(8,128)S(1)}, u32[]{:S(2)}, u32[]{:S(2)}) collective-permute-start(f32[384,1152]{1,0:T(8,128)S(1)} %add.228), channel_id=1, source_target_pairs={{0,4},{4,8},{8,12},{12,16},{16,20},{20,24},{24,28},{28,32},{32,36}... | collective-permute-start | bytes 5308424 | tf_op jit(solution)/shard_map/ppermute | solution.py:9
  307.1 60.6 %collective-permute-start.3 = (bf16[384,1152]{1,0:T(8,128)(2,1)S(1)}, bf16[384,1152]{1,0:T(8,128)(2,1)S(1)}, u32[]{:S(2)}, u32[]{:S(2)}) collective-permute-start(bf16[384,1152]{1,0:T(8,128)(2,1)S(1)} %collective-permute-done.2), channel_id=1, source_target_pairs={{0,4},{4,8},{8,12},{12,16},{16,20},{20,24},{24,28},{28,32},{32,36}... | collective-permute-start | bytes 2654216 | tf_op jit(solution)/shard_map/ppermute | solution.py:9
  369.5 62.7 %collective-permute-start.11 = (f32[384,1152]{1,0:T(8,128)S(1)}, f32[384,1152]{1,0:T(8,128)S(1)}, u32[]{:S(2)}, u32[]{:S(2)}) collective-permute-start(f32[384,1152]{1,0:T(8,128)S(1)} %add.229), channel_id=1, source_target_pairs={{0,4},{4,8},{8,12},{12,16},{16,20},{20,24},{24,28},{28,32},{32,36}... | collective-permute-start | bytes 5308424 | tf_op jit(solution)/shard_map/ppermute | solution.py:9
  369.6 59.8 %collective-permute-start.4 = (bf16[384,1152]{1,0:T(8,128)(2,1)S(1)}, bf16[384,1152]{1,0:T(8,128)(2,1)}, u32[]{:S(2)}, u32[]{:S(2)}) collective-permute-start(bf16[384,1152]{1,0:T(8,128)(2,1)S(1)} %collective-permute-done.3), channel_id=1, source_target_pairs={{0,4},{4,8},{8,12},{12,16},{16,20},{20,24},{24,28},{28,32},{32,36}... | collective-permute-start | bytes 2654216 | tf_op jit(solution)/shard_map/ppermute | solution.py:9
  433.6 61.9 %collective-permute-start.12 = (f32[384,1152]{1,0:T(8,128)}, f32[384,1152]{1,0:T(8,128)}, u32[]{:S(2)}, u32[]{:S(2)}) collective-permute-start(f32[384,1152]{1,0:T(8,128)} %add.230), channel_id=1, source_target_pairs={{0,4},{4,8},{8,12},{12,16},{16,20},{20,24},{24,28},{28,32},{32,36}... | collective-permute-start | bytes 5308424 | tf_op jit(solution)/shard_map/ppermute | solution.py:9
  433.6 59.1 %collective-permute-start.5 = (bf16[384,1152]{1,0:T(8,128)(2,1)}, bf16[384,1152]{1,0:T(8,128)(2,1)}, u32[]{:S(2)}, u32[]{:S(2)}) collective-permute-start(bf16[384,1152]{1,0:T(8,128)(2,1)} %collective-permute-done.4), channel_id=1, source_target_pairs={{0,4},{4,8},{8,12},{12,16},{16,20},{20,24},{24,28},{28,32},{32,36}... | collective-permute-start | bytes 2654216 | tf_op jit(solution)/shard_map/ppermute | solution.py:9
  436.7 57.9 %slice-start = ((s8[4718592]{0:T(1024)(128)(4,1)}), s8[4194304]{0:T(1024)(128)(4,1)S(1)}, s32[]{:S(2)}) async-start(s8[4718592]{0:T(1024)(128)(4,1)} %bitcast.60), calls=%async_computation.1 | async-start | bytes 8388608
  439.9 54.7 %slice-start.1 = ((s8[4718592]{0:T(1024)(128)(4,1)}), s8[524288]{0:T(1024)(128)(4,1)S(1)}, s32[]{:S(2)}) async-start(s8[4718592]{0:T(1024)(128)(4,1)} %bitcast.60), calls=%async_computation.2 | async-start | bytes 1048576
  492.7 27.0 %collective-permute-start.6 = (bf16[384,1152]{1,0:T(8,128)(2,1)}, bf16[384,1152]{1,0:T(8,128)(2,1)S(1)}, u32[]{:S(2)}, u32[]{:S(2)}) collective-permute-start(bf16[384,1152]{1,0:T(8,128)(2,1)} %collective-permute-done.5), channel_id=1, source_target_pairs={{0,4},{4,8},{8,12},{12,16},{16,20},{20,24},{24,28},{28,32},{32,36}... | collective-permute-start | bytes 2654216 | tf_op jit(solution)/shard_map/ppermute | solution.py:9
  494.6 25.2 %copy-start.26 = (f32[384,384]{1,0:T(8,128)}, f32[384,384]{1,0:T(8,128)S(1)}, u32[]{:S(2)}) copy-start(f32[384,384]{1,0:T(8,128)S(1)} %fusion.1) | copy-start | bytes 1769476
  497.3 66.2 %collective-permute-start.13 = (f32[384,1152]{1,0:T(8,128)S(1)}, f32[384,1152]{1,0:T(8,128)S(1)}, u32[]{:S(2)}, u32[]{:S(2)}) collective-permute-start(f32[384,1152]{1,0:T(8,128)S(1)} %add.231), channel_id=1, source_target_pairs={{0,4},{4,8},{8,12},{12,16},{16,20},{20,24},{24,28},{28,32},{32,36}... | collective-permute-start | bytes 5308424 | tf_op jit(solution)/shard_map/ppermute | solution.py:9
  498.7 21.1 %copy-start.25 = (f32[384,384]{1,0:T(8,128)S(1)}, f32[384,384]{1,0:T(8,128)}, u32[]{:S(2)}) copy-start(f32[384,384]{1,0:T(8,128)} %copy-done.24) | copy-start | bytes 1769476
  564.9 176.4 %collective-permute-start.14 = (f32[384,1152]{1,0:T(8,128)}, f32[384,1152]{1,0:T(8,128)}, u32[]{:S(2)}, u32[]{:S(2)}) collective-permute-start(f32[384,1152]{1,0:T(8,128)} %add.232), channel_id=1, source_target_pairs={{0,228},{4,232},{8,236},{12,240},{16,244},{20,248},{24,252},{28,0}... | collective-permute-start | bytes 5308424 | tf_op jit(solution)/shard_map/ppermute | solution.py:9
  571.9 164.5 %copy-start.13 = (bf16[384,1152]{1,0:T(8,128)(2,1)S(1)}, bf16[384,1152]{1,0:T(8,128)(2,1)}, u32[]{:S(2)}) copy-start(bf16[384,1152]{1,0:T(8,128)(2,1)} %copy-done.12) | copy-start | bytes 2654212
  (23 other events, 47.6 us)
Sparse Core Ops, SparseCore 0:
  13.2 87.3 all-reduce.2
where the time goes:
time: 755 us; the launch traced here: 754 us
  waiting for transfers between devices  509 us (67%)
  blocking collectives  159 us (21%)
  matrix products  48.2 us (6%)
  between operations  22.7 us (3%)
  other arithmetic  9.51 us (1%)
    ppermute x15, waiting for transfers between devices, from_behind(): return lax.ppermute(x, axis, [(i, (i + by) % peers) for i in range(peers)])  422 us
    psum x1, blocking collectives, on_device(): total = lax.psum(loss_sum, 'batch')  159 us
    psum x1, waiting for transfers between devices, on_device(): pre_p, pre_r = lax.psum((part_p, part_r), 'tower')  86.1 us
    dot_general x8, matrix products, on_device(): jnp.dot(coef, current, preferred_element_type=jnp.float32)  19.8 us
  transfers between devices with their start and end apart: 16, of which 10 were waited for; matrix products, arithmetic and copies ran while one was open for 5% of the time, Pallas kernels for 0%

commit v1 on v0

v1 whole, which is shorter than its diff:
```python
import jax
import jax.numpy as jnp
from jax import lax
from jax.experimental import pallas as pl
from jax.experimental.pallas import tpu as pltpu
from jax.sharding import PartitionSpec as P

BF, F32 = jnp.bfloat16, jnp.float32
ROWS, FEAT, EMB, STEPS, BLOCKS, TOWER = 384, 288, 1152, 8, 64, 4
HALF, QUART = ROWS // 2, ROWS // 4
SLOTS = 5
NT = (((1,), (1,)), ((), ()))
TN = (((0,), (0,)), ((), ()))


def dot(a, b, dims=(((1,), (0,)), ((), ()))):
    return lax.dot_general(a, b, dims, preferred_element_type=F32)


def sigmoid(x):
    e = jnp.exp(-jnp.abs(x))
    return jnp.where(x >= 0, 1.0, e) / (1.0 + e)


def kernel(
    feats_r, feats_p, proj_r, proj_p, scale_ref, bias_ref, teach, valid,
    out_r, out_p, loss_ref,
    projs, feat_f, feat_n, fsend, frecv, unit, norm, emb_p, emb_r,
    traw, tsend, trecv, target, vown, vother, gp, gr, gpsend, gprecv,
    grsib_s, grsib_r, grsend, grrecv, dsend, dbuf, osend, oval,
    lmsg, lbuf, send_sem, recv_sem, loc_sem,
):
    b = lax.axis_index("batch")
    t = lax.axis_index("tower")
    l = lax.rem(b, 2)
    h, c = t // 2, lax.rem(t, 2)
    nb = b + 1 - 2 * l
    st = t + 1 - 2 * c
    ft = lax.rem(t + 2, TOWER)

    def dev(batch, tower):
        return {"batch": batch, "tower": tower}

    SIB, NEAR, NEARX, FAR = dev(b, st), dev(nb, t), dev(nb, st), dev(nb, ft)

    def ahead(i):
        return dev(lax.rem(b + 2 * i, BLOCKS), t)

    def behind(i):
        return dev(lax.rem(b + BLOCKS - 2 * i, BLOCKS), t)

    plane = (b // 8) * 8
    inplane = b - plane
    group_id = l * TOWER + t

    def group_peer(k):
        g = lax.rem(group_id + k, 8)
        return dev(b - l + g // TOWER, lax.rem(g, TOWER))

    def y_peer(k):
        return dev(plane + lax.rem(inplane + 2 * k, 8), t)

    def z_peer(k):
        return dev(lax.rem(b + 8 * k, BLOCKS), t)

    barrier = pltpu.get_barrier_semaphore()
    peers = [group_peer(k) for k in range(1, 8)]
    peers += [ahead(i) for i in range(1, SLOTS)] + [behind(i) for i in range(1, SLOTS)]
    peers += [y_peer(k) for k in range(1, 4)] + [z_peer(k) for k in range(2, 7)]
    for peer in peers:
        pl.semaphore_signal(barrier, inc=1, device_id=peer, device_id_type=pl.DeviceIdType.MESH)

    def quarter(half, core):
        return pl.ds(pl.multiple_of(half * HALF + core * QUART, 32), QUART)

    def part(core):
        return pl.ds(pl.multiple_of(core * QUART, 32), QUART)

    feats, proj = (feats_r, feats_p), (proj_r, proj_p)
    count = [0]
    local = []

    def load(src, dst):
        copy = pltpu.make_async_copy(src, dst, loc_sem.at[len(local)])
        copy.start()
        local.append(copy)
        return copy

    sends = []

    def remote(src, dst, to, start=True):
        k = count[0]
        count[0] += 1
        copy = pltpu.make_async_remote_copy(
            src_ref=src, dst_ref=dst, send_sem=send_sem.at[k], recv_sem=recv_sem.at[k],
            device_id=to, device_id_type=pl.DeviceIdType.MESH,
        )
        if start:
            copy.start()
            sends.append(copy)
        return copy

    own_proj, own_feat = [], []
    for w in (0, 1):
        own_proj.append(load(proj[w], projs.at[w, 0]))
        own_feat.append(load(feats[w].at[quarter(1 - h, c)], feat_f.at[w, 0]))
    own_teach = [load(teach.at[quarter(hh, c)], traw.at[hh]) for hh in (0, 1)]
    own_valid = [load(valid.at[quarter(hh, c)], vown.at[hh]) for hh in (0, 1)]

    pl.semaphore_wait(barrier, len(peers))

    to_sib, feat_sib, feat_near, feat_nearx = [], [], [], []
    for w in (0, 1):
        feat_sib.append(remote(feats[w].at[quarter(1 - h, 1 - c)], feat_f.at[w, 1], SIB))
        to_sib.append(remote(proj[w], projs.at[w, 1], SIB))
        feat_near.append(remote(feats[w].at[quarter(h, c)], feat_n.at[w, 0], NEAR))
        feat_nearx.append(remote(feats[w].at[quarter(h, 1 - c)], feat_n.at[w, 1], NEARX))
    valid_near = [remote(valid.at[quarter(hh, c)], vother.at[hh], NEAR) for hh in (0, 1)]

    partial = []
    for w in (0, 1):
        own_proj[w].wait()
        own_feat[w].wait()
        acc = dot(feat_f[w, 0], projs[w, 0])
        feat_sib[w].wait_recv()
        to_sib[w].wait_recv()
        acc += dot(feat_f[w, 1], projs[w, 1])
        fsend[w] = acc.astype(BF)
        partial.append(remote(fsend.at[w], frecv.at[w], FAR))

    for copy in own_teach:
        copy.wait()

    def steps_of(hh, s):
        both = traw[hh, :, s * ROWS:(s + 1) * ROWS].astype(F32)
        return jnp.where(h == 0, both, pltpu.roll(both, HALF, 1))[:, :HALF]

    for hh in (0, 1):
        for q in range(4):
            tsend[q, hh * QUART:(hh + 1) * QUART] = steps_of(hh, 2 * q).astype(BF)
    teach_near = remote(tsend, trecv, NEAR)

    def finish(w):
        feat_near[w].wait_recv()
        feat_nearx[w].wait_recv()
        pre = dot(feat_n[w, 0], projs[w, 0]) + dot(feat_n[w, 1], projs[w, 1])
        partial[w].wait_recv()
        pre = pre + frecv[w].astype(F32)
        length = jnp.sqrt(jnp.sum(pre * pre, axis=1, keepdims=True) + 1e-06)
        norm[w] = jnp.broadcast_to(length, (QUART, 128))
        u = pre / length
        unit[w] = u
        return u.astype(BF)

    emb_r[0, part(c)] = finish(0)
    band = [None] * SLOTS
    for i in (3, 2, 1):
        band[i] = remote(emb_r.at[0, part(c)], emb_r.at[i, part(c)], ahead(i))
    band[4] = remote(emb_r.at[0, part(c)], emb_r.at[4, part(c)], ahead(4), start=False)

    @pl.when(l == 0)
    def _():
        band[4].start()

    resp_sib = [None] * SLOTS
    resp_sib[0] = remote(emb_r.at[0, part(c)], emb_r.at[0, part(c)], SIB)

    emb_p[0, part(h)] = finish(1)
    p_far = remote(emb_p.at[0, part(h)], emb_p.at[1, part(h)], FAR)
    p_near = remote(emb_p.at[0, part(h)], emb_p.at[1, part(h)], NEAR)

    for hh in (0, 1):
        for q in range(4):
            target[1, q, hh * QUART:(hh + 1) * QUART] = sigmoid(steps_of(hh, 2 * q + 1) / 32.0)

    p_far.wait_recv()
    p_opp = remote(emb_p.at[1, part(1 - h)], emb_p.at[0, part(1 - h)], NEAR)

    teach_near.wait_recv()
    for q in range(4):
        target[0, q] = sigmoid(trecv[q].astype(F32) / 32.0)

    for i in (1, 2, 3):
        band[i].wait_recv()
        resp_sib[i] = remote(emb_r.at[i, part(c)], emb_r.at[i, part(c)], SIB)
    resp_sib[4] = remote(emb_r.at[4, part(c)], emb_r.at[4, part(c)], SIB, start=False)

    @pl.when(l == 0)
    def _():
        band[4].wait_recv()
        resp_sib[4].start()

    for hh in (0, 1):
        own_valid[hh].wait()
        valid_near[hh].wait_recv()
    p_near.wait_recv()
    p_opp.wait_recv()
    for i in (3, 2, 1, 0):
        resp_sib[i].wait_recv()

    @pl.when(l == 0)
    def _():
        resp_sib[4].wait_recv()

    scale, bias = scale_ref[0], bias_ref[0]
    loss = jnp.zeros((8, HALF), F32)
    gr_sib, gr_home = [None] * SLOTS, [None] * SLOTS

    def push(i, slot):
        grsib_s[i] = gr[slot, part(1 - c)].astype(BF)

    for q in (3, 2, 1, 0):
        for kind in (0, 1):
            slot = q if kind == 0 else q + 1 - l
            weight = (vother if kind == 0 else vown)[:, :, 2 * q + kind:2 * q + kind + 1]
            weight = weight.reshape(HALF, 1).astype(F32)
            goal = target[kind, q]
            z = scale * dot(emb_p[kind], emb_r[slot], NT) + bias
            e = jnp.exp(-jnp.abs(z))
            soft = jnp.maximum(z, 0.0) + jnp.log1p(e)
            sig = jnp.where(z >= 0, 1.0, e) / (1.0 + e)
            cost = weight * (soft - goal * z)
            loss = loss + jnp.sum(cost.reshape(HALF // 8, 8, HALF), axis=0)
            coef = (scale * weight * (sig - goal)).astype(BF)
            term_p = dot(coef, emb_r[slot])
            term_r = dot(coef, emb_p[kind], TN)
            if q == 3:
                gp[kind] = term_p
            else:
                gp[kind] += term_p
            if kind == 0:
                gr[q] = term_r
            elif q == 3:
                @pl.when(l == 0)
                def _():
                    gr[4] = term_r

                @pl.when(l == 1)
                def _():
                    gr[3] += term_r
            else:
                gr[slot] += term_r

    gpsend[0] = gp[0, part(1 - h)].astype(BF)
    g_opp = remote(gpsend.at[0], gprecv.at[0], NEAR)
    for i in (3, 2, 1, 0):
        push(i, i)
        gr_sib[i] = remote(grsib_s.at[i], grsib_r.at[i], SIB)
    gr_sib[4] = remote(grsib_s.at[4], grsib_r.at[4], SIB, start=False)

    @pl.when(l == 0)
    def _():
        push(4, 4)
        gr_sib[4].start()

    gpsend[1] = gp[1, part(h)].astype(BF)
    g_near = remote(gpsend.at[1], gprecv.at[1], NEAR)

    for i in (3, 2, 1):
        gr_sib[i].wait_recv()
        grsend[i] = (gr[i, part(c)] + grsib_r[i].astype(F32)).astype(BF)
        gr_home[i] = remote(grsend.at[i], grrecv.at[i], behind(i))
    gr_home[4] = remote(grsend.at[4], grrecv.at[4], behind(4), start=False)

    @pl.when(l == 0)
    def _():
        gr_sib[4].wait_recv()
        grsend[4] = (gr[4, part(c)] + grsib_r[4].astype(F32)).astype(BF)
        gr_home[4].start()

    g_opp.wait_recv()
    gpsend[2] = (gp[1, part(1 - h)] + gprecv[0].astype(F32)).astype(BF)
    g_far = remote(gpsend.at[2], gprecv.at[2], FAR)

    def gather(stage, value, me, total, peer_of):
        lmsg[stage] = jnp.full((8, 128), value, F32)
        lbuf[stage, me] = lmsg[stage]
        copies = [remote(lmsg.at[stage], lbuf.at[stage, me], peer_of(k)) for k in range(1, total)]
        for copy in copies:
            copy.wait_recv()
        return jnp.sum(lbuf[stage, :total]) / 1024.0

    total = gather(0, jnp.sum(loss), group_id, 8, group_peer)
    total = gather(1, total, inplane // 2, 4, y_peer)
    total = gather(2, total, b // 8, 8, z_peer)
    loss_ref[0] = total / (ROWS * BLOCKS * STEPS * ROWS)

    d_far, d_sib, o_near, o_nearx = [None] * 2, [None] * 2, [None] * 2, [None] * 2

    def back(w, g):
        u = unit[w]
        inner = jnp.sum(u * g, axis=1, keepdims=True)
        d = ((g - u * inner) / norm[w, :, 0:1]).astype(BF)
        dsend[w] = d
        d_far[w] = remote(dsend.at[w], dbuf.at[w, part(c)], FAR)
        osend[w, 0] = dot(d, projs[w, 0], NT).astype(BF)
        osend[w, 1] = dot(d, projs[w, 1], NT).astype(BF)
        o_near[w] = remote(osend.at[w, 0], oval.at[w, h, part(c)], NEAR)
        o_nearx[w] = remote(osend.at[w, 1], oval.at[w, h, part(c)], NEARX)

    g_near.wait_recv()
    g_far.wait_recv()
    back(1, gp[0, part(h)] + gprecv[1].astype(F32) + gprecv[2].astype(F32))

    gr_sib[0].wait_recv()
    gr[0, part(c)] += grsib_r[0].astype(F32)
    for i in (1, 2, 3):
        gr_home[i].wait_recv()
        gr[0, part(c)] += grrecv[i].astype(F32)

    @pl.when(l == 0)
    def _():
        gr_home[4].wait_recv()
        gr[0, part(c)] += grrecv[4].astype(F32)

    back(0, gr[0, part(c)])

    outs = (out_r, out_p)
    for w in (1, 0):
        d_far[w].wait_recv()
        d_sib[w] = remote(dbuf.at[w, part(c)], dbuf.at[w, part(c)], SIB)
    for w in (1, 0):
        d_sib[w].wait_recv()
        oval[w, 1 - h] = dot(dbuf[w], projs[w, 0], NT).astype(BF)
        o_near[w].wait_recv()
        o_nearx[w].wait_recv()
        for hh in (0, 1):
            load(oval.at[w, hh], outs[w].at[hh * HALF:(hh + 1) * HALF])
    for copy in local[-4:]:
        copy.wait()
    for copy in sends:
        copy.wait_send()

    @pl.when(l == 0)
    def _():
        for copy in (band[4], resp_sib[4], gr_sib[4], gr_home[4]):
            copy.wait_send()


def on_device(
    prompt_feats, response_feats, prompt_proj, response_proj,
    logit_scale, logit_bias, teacher, valid,
):
    anywhere = pl.BlockSpec(memory_space=pl.ANY)
    scalar = pl.BlockSpec(memory_space=pltpu.SMEM)

    def vm(*shape, kind=BF):
        return pltpu.VMEM(shape, kind)

    grad_response, grad_prompt, loss = pl.pallas_call(
        kernel,
        out_shape=(
            jax.ShapeDtypeStruct((ROWS, FEAT), BF),
            jax.ShapeDtypeStruct((ROWS, FEAT), BF),
            jax.ShapeDtypeStruct((1,), F32),
        ),
        in_specs=[anywhere] * 4 + [scalar] * 2 + [anywhere] * 2,
        out_specs=(anywhere, anywhere, scalar),
        scratch_shapes=[
            vm(2, 2, FEAT, EMB),
            vm(2, 2, QUART, FEAT),
            vm(2, 2, QUART, FEAT),
            vm(2, QUART, EMB),
            vm(2, QUART, EMB),
            vm(2, QUART, EMB, kind=F32),
            vm(2, QUART, 128, kind=F32),
            vm(2, HALF, EMB),
            vm(SLOTS, HALF, EMB),
            vm(2, QUART, STEPS * ROWS, kind=jnp.int32),
            vm(4, HALF, HALF),
            vm(4, HALF, HALF),
            vm(2, 4, HALF, HALF, kind=F32),
            vm(2, QUART, STEPS, kind=jnp.int32),
            vm(2, QUART, STEPS, kind=jnp.int32),
            vm(2, HALF, EMB, kind=F32),
            vm(SLOTS, HALF, EMB, kind=F32),
            vm(3, QUART, EMB),
            vm(3, QUART, EMB),
            vm(SLOTS, QUART, EMB),
            vm(SLOTS, QUART, EMB),
            vm(SLOTS, QUART, EMB),
            vm(SLOTS, QUART, EMB),
            vm(2, QUART, EMB),
            vm(2, HALF, EMB),
            vm(2, 2, QUART, FEAT),
            vm(2, 2, HALF, FEAT),
            vm(3, 8, 128, kind=F32),
            vm(3, 8, 8, 128, kind=F32),
            pltpu.SemaphoreType.DMA((64,)),
            pltpu.SemaphoreType.DMA((64,)),
            pltpu.SemaphoreType.DMA((16,)),
        ],
        compiler_params=pltpu.CompilerParams(
            collective_id=0, has_side_effects=True, vmem_limit_bytes=56 * 2**20
        ),
        name="band",
    )(
        response_feats, prompt_feats, response_proj, prompt_proj,
        logit_scale, logit_bias, teacher, valid,
    )
    return grad_prompt, grad_response, loss


def solution(mesh):
    in_specs = (
        P("batch", "tower"), P("batch", "tower"), P("tower", None), P("tower", None),
        P(), P(), P("batch", None), P("batch", None),
    )
    out_specs = (P("batch", "tower"), P("batch", "tower"), P())
    return jax.shard_map(
        on_device, mesh=mesh, in_specs=in_specs, out_specs=out_specs, check_vma=False
    )
```

time: 755 us -> 97.8 us (0.13)
  the two profiles are of different devices: /device:TPU:4 before, /device:TPU:1 now
where the time goes in v1:
time: 97.8 us; the launch traced here: 96.7 us
  Pallas kernels  84.2 us (86%)
  local copies, waits for them, and re-layouts  8.73 us (9%)
  between operations  3.68 us (4%)
    pallas_call x1, Pallas kernels, on_device(): pl.pallas_call(kernel, out_shape=(jax.ShapeDtypeStruct((ROWS, FEAT), BF),...  84.2 us
    unnamed x5, local copies, waits for them, and re-layouts  8.73 us

profile of v1, /device:TPU:1, one launch (start us, length us, event | category | flops | bytes accessed | tf_op | source)
XLA Modules:
  0.0 96.7 jit_solution(5873148309704289041)
XLA Ops:
  1.9 1.5 %copy.13.valid = s32[384,8]{1,0:T(8,128)} copy(s32[384,8]{0,1:T(8,128)} %param.15) | data formatting | bytes 24576 | tf_op args[7]
  3.4 1.8 %copy.12.feats_p = bf16[384,288]{1,0:T(8,128)(2,1)} copy(bf16[384,288]{0,1:T(8,128)(2,1)} %param.8) | data formatting | bytes 442368 | tf_op args[0]
  5.3 1.8 %copy.11.feats_r = bf16[384,288]{1,0:T(8,128)(2,1)} copy(bf16[384,288]{0,1:T(8,128)(2,1)} %param.9) | data formatting | bytes 442368 | tf_op args[1]
  7.1 84.2 %band.1 = (bf16[384,288]{1,0:T(8,128)(2,1)}, bf16[384,288]{1,0:T(8,128)(2,1)}, f32[1]{0:T(128)}) custom-call(bf16[384,288]{1,0:T(8,128)(2,1)} %copy.11.feats_r, bf16[384,288]{1,0:T(8,128)(2,1)} %copy.12.feats_p, bf16[288,1152]{1,0:T(8,128)(2,1)} %proj_r.1, bf16[288,1152]{1,0:T(8,128)(2,1)} %proj_p.1, f32[1]{0:T(128)S(6)} %copy.17.scale_ref, ...), custom_call_target="tpu_custom_call" | custom-call | tf_op jit(solution)/shard_map/band/pallas_call | solution.py:350
  91.3 1.8 %copy.14 = bf16[384,288]{0,1:T(8,128)(2,1)} copy(bf16[384,288]{1,0:T(8,128)(2,1)} %get-tuple-element.9) | data formatting | bytes 442368
  93.1 1.8 %copy.15 = bf16[384,288]{0,1:T(8,128)(2,1)} copy(bf16[384,288]{1,0:T(8,128)(2,1)} %get-tuple-element.10) | data formatting | bytes 442368

commit v2 on v1

v2 whole, which is shorter than its diff:
```python
import jax
import jax.numpy as jnp
from jax import lax
from jax.experimental import pallas as pl
from jax.experimental.pallas import tpu as pltpu
from jax.sharding import PartitionSpec as P

BF, F32 = jnp.bfloat16, jnp.float32
ROWS, FEAT, EMB, STEPS, BLOCKS, TOWER = 384, 288, 1152, 8, 64, 4
HALF, QUART = ROWS // 2, ROWS // 4
SLOTS, PIECE = 5, 48
NT = (((1,), (1,)), ((), ()))
TN = (((0,), (0,)), ((), ()))


def dot(a, b, dims=(((1,), (0,)), ((), ()))):
    return lax.dot_general(a, b, dims, preferred_element_type=F32)


def sigmoid(x):
    e = jnp.exp(-jnp.abs(x))
    return jnp.where(x >= 0, 1.0, e) / (1.0 + e)


def kernel(
    feats_r, feats_p, proj_r, proj_p, scale_ref, bias_ref, teach, valid,
    out_r, out_p, loss_ref,
    fcols, frows, projs, feat_f, feat_n, fsend, frecv, unit, norm, emb_p, emb_r,
    traw, tsend, trecv, target, vcols, vrows, gp, gr, gpsend, gprecv,
    grsib_s, grsib_r, grsend, grrecv, dsend, dbuf, osend, onear, oval,
    lmsg, lbuf, send_sem, recv_sem, loc_sem,
):
    b = lax.axis_index("batch")
    t = lax.axis_index("tower")
    l = lax.rem(b, 2)
    h, c = t // 2, lax.rem(t, 2)
    nb = b + 1 - 2 * l
    st = t + 1 - 2 * c
    ft = lax.rem(t + 2, TOWER)
    plane = (b // 8) * 8
    inplane = b - plane
    y = inplane // 2
    odd = lax.rem(y, 2)

    def dev(batch, tower):
        return {"batch": batch, "tower": tower}

    SIB, NEAR, NEARX, FAR = dev(b, st), dev(nb, t), dev(nb, st), dev(nb, ft)
    UP, DOWN = dev(plane + lax.rem(inplane + 2, 8), t), dev(plane + lax.rem(inplane + 6, 8), t)
    PAIR = dev(b + 2 - 4 * odd, t)
    AHEAD, BEHIND = dev(lax.rem(b + 8, BLOCKS), t), dev(lax.rem(b + BLOCKS - 8, BLOCKS), t)
    group_id = l * TOWER + t

    def group_peer(k):
        g = lax.rem(group_id + k, 8)
        return dev(b - l + g // TOWER, lax.rem(g, TOWER))

    def y_peer(k):
        return dev(plane + lax.rem(inplane + 2 * k, 8), t)

    def z_peer(k):
        return dev(lax.rem(b + 8 * k, BLOCKS), t)

    barrier = pltpu.get_barrier_semaphore()
    peers = [group_peer(k) for k in range(1, 8)]
    peers += [y_peer(k) for k in range(1, 4)] + [z_peer(k) for k in range(1, 8)]
    for peer in peers:
        pl.semaphore_signal(barrier, inc=1, device_id=peer, device_id_type=pl.DeviceIdType.MESH)

    def rows_at(start, count):
        return pl.ds(pl.multiple_of(start, 16), count)

    def quarter(half, core):
        return rows_at(half * HALF + core * QUART, QUART)

    def part(core):
        return rows_at(core * QUART, QUART)

    def piece(slot, core, k):
        return rows_at(slot * HALF + core * QUART + k * PIECE, PIECE)

    def cut(k):
        return slice(k * PIECE, (k + 1) * PIECE)

    feats, proj = (feats_r, feats_p), (proj_r, proj_p)
    local = []

    def load(src, dst):
        copy = pltpu.make_async_copy(src, dst, loc_sem.at[len(local)])
        copy.start()
        local.append(copy)
        return copy

    links = []

    class Link:
        def __init__(self, copy):
            self.copy, self.waited = copy, False

        def start(self):
            self.copy.start()

        def wait_recv(self):
            self.waited = True
            self.copy.wait_recv()

    def remote(src, dst, to, start=True):
        k = len(links)
        link = Link(
            pltpu.make_async_remote_copy(
                src_ref=src, dst_ref=dst, send_sem=send_sem.at[k], recv_sem=recv_sem.at[k],
                device_id=to, device_id_type=pl.DeviceIdType.MESH,
            )
        )
        if start:
            link.start()
        links.append(link)
        return link

    def close():
        for link in links:
            if not link.waited:
                link.copy.wait_recv()
            link.copy.wait_send()

    own_feat = [load(feats[w], fcols.at[w]) for w in (0, 1)]
    own_proj = [load(proj[w], projs.at[w, 0]) for w in (0, 1)]
    own_teach = [load(teach.at[quarter(hh, c)], traw.at[hh]) for hh in (0, 1)]
    own_valid = load(valid, vcols.at[1])

    for w in (0, 1):
        own_feat[w].wait()
        frows[w] = fcols[w].astype(F32).T.astype(BF)
    pl.semaphore_wait(barrier, len(peers))

    to_sib, feat_sib, feat_near, feat_nearx = [], [], [], []

    def enter(w):
        feat_sib.append(remote(frows.at[w, quarter(1 - h, 1 - c)], feat_f.at[w], SIB))
        to_sib.append(remote(proj[w], projs.at[w, 1], SIB))
        feat_near.append(remote(frows.at[w, quarter(h, c)], feat_n.at[w, 0], NEAR))
        feat_nearx.append(remote(frows.at[w, quarter(h, 1 - c)], feat_n.at[w, 1], NEARX))

    partial = []

    def half_sum(w):
        own_proj[w].wait()
        acc = dot(frows[w, quarter(1 - h, c)], projs[w, 0])
        feat_sib[w].wait_recv()
        to_sib[w].wait_recv()
        acc += dot(feat_f[w], projs[w, 1])
        fsend[w] = acc.astype(BF)
        partial.append(remote(fsend.at[w], frecv.at[w], FAR))

    enter(0)
    own_proj[0].wait()
    first = dot(frows[0, quarter(1 - h, c)], projs[0, 0])
    feat_sib[0].wait_recv()
    to_sib[0].wait_recv()
    enter(1)
    fsend[0] = (first + dot(feat_f[0], projs[0, 1])).astype(BF)
    partial.append(remote(fsend.at[0], frecv.at[0], FAR))
    half_sum(1)

    for copy in own_teach:
        copy.wait()
    early = lax.broadcasted_iota(jnp.int32, (1, ROWS), 1) < HALF

    def steps_of(hh, s):
        a = traw[hh, :, s * ROWS:(s + 1) * ROWS].astype(F32)
        d = traw[hh, :, (s + 2) * ROWS:(s + 3) * ROWS].astype(F32)
        keep = jnp.where(h == 0, a, d)
        turn = pltpu.roll(jnp.where(h == 0, d, a), HALF, 1)
        lanes = lax.broadcasted_iota(jnp.int32, (QUART, ROWS), 1)
        return jnp.where((lanes < HALF) == (h == 0), keep, turn)

    for p in (0, 1):
        for hh in (0, 1):
            tsend[p, hh * QUART:(hh + 1) * QUART] = steps_of(hh, 4 * p).astype(BF)
    teach_near = remote(tsend, trecv, NEAR)
    valid_near = remote(valid, vcols.at[0], NEAR)
    for p in (0, 1):
        for hh in (0, 1):
            target[1, p, hh * QUART:(hh + 1) * QUART] = sigmoid(steps_of(hh, 4 * p + 1) / 32.0)
    gr[4 * HALF:] = jnp.zeros((HALF, EMB), F32)

    def finish(w):
        feat_near[w].wait_recv()
        feat_nearx[w].wait_recv()
        pre = dot(feat_n[w, 0], projs[w, 0]) + dot(feat_n[w, 1], projs[w, 1])
        partial[w].wait_recv()
        pre = pre + frecv[w].astype(F32)
        length = jnp.sqrt(jnp.sum(pre * pre, axis=1, keepdims=True) + 1e-06)
        norm[w] = jnp.broadcast_to(length, (QUART, 128))
        u = pre / length
        unit[w] = u
        return u.astype(BF)

    pieces = range(ROWS // 4 // PIECE)
    up_from, down_from, pair_from = (y // 3) * 4, ((y + 3) // 4) * 4, 1 + 2 * odd

    def relay(src, dst, to, start=True):
        return [
            remote(emb_r.at[piece(src, c, k)], emb_r.at[piece(dst, c, k)], to, start)
            for k in pieces
        ]

    def resp_over(slot):
        at = quarter(slot, c)
        return remote(emb_r.at[at], emb_r.at[at], SIB)

    emb_r[part(c)] = finish(0)
    zhop = relay(0, 4, AHEAD)
    up, down = relay(up_from, 1, UP, False), relay(down_from, 3, DOWN, False)
    pair = relay(pair_from, 2, PAIR, False)

    @pl.when(y < 3)
    def _():
        for link in up:
            link.start()

    @pl.when(y == 0)
    def _():
        for link in down:
            link.start()

    resp_sib = [None] * SLOTS
    resp_sib[0] = resp_over(0)

    fresh = finish(1)
    emb_p[0, part(h)] = fresh
    p_far, p_near, p_opp = [], [], []
    for k in pieces:
        at = rows_at(h * QUART + k * PIECE, PIECE)
        p_far.append(remote(emb_p.at[0, at], emb_p.at[1, at], FAR))
        p_near.append(remote(emb_p.at[0, at], emb_p.at[1, at], NEAR))

    for k in pieces:
        zhop[k].wait_recv()

        @pl.when(y == 3)
        def _():
            up[k].start()

        @pl.when(y > 0)
        def _():
            down[k].start()

    resp_sib[4] = resp_over(4)

    teach_near.wait_recv()
    for p in (0, 1):
        target[0, p] = sigmoid(trecv[p].astype(F32) / 32.0)
    own_valid.wait()
    valid_near.wait_recv()
    for kind in (0, 1):
        vrows[kind] = vcols[kind].astype(F32).T

    for k in pieces:
        @pl.when(odd == 0)
        def _():
            up[k].wait_recv()

        @pl.when(odd == 1)
        def _():
            down[k].wait_recv()

        pair[k].start()
        p_far[k].wait_recv()
        at = rows_at((1 - h) * QUART + k * PIECE, PIECE)
        p_opp.append(remote(emb_p.at[1, at], emb_p.at[0, at], NEAR))

    for k in pieces:
        @pl.when(odd == 1)
        def _():
            up[k].wait_recv()

        @pl.when(odd == 0)
        def _():
            down[k].wait_recv()

    resp_sib[3], resp_sib[1] = resp_over(3), resp_over(1)
    for k in pieces:
        pair[k].wait_recv()
    resp_sib[2] = resp_over(2)
    for k in pieces:
        p_near[k].wait_recv()
        p_opp[k].wait_recv()
    for i in (4, 3, 2, 1, 0):
        resp_sib[i].wait_recv()

    scale, bias = scale_ref[0], bias_ref[0]
    loss = jnp.zeros((8, ROWS), F32)
    for p in (1, 0):
        for kind in (0, 1):
            slots = pl.ds(pl.multiple_of((2 * p + kind * (1 - l)) * HALF, 64), ROWS)
            step = 4 * p + kind
            weight = jnp.concatenate(
                [
                    jnp.where(
                        early,
                        vrows[kind, quarter(hh, c), step:step + 1],
                        vrows[kind, quarter(hh, c), step + 2:step + 3],
                    )
                    for hh in (0, 1)
                ],
                axis=0,
            )
            goal = target[kind, p]
            z = scale * dot(emb_p[kind], emb_r[slots], NT) + bias
            e = jnp.exp(-jnp.abs(z))
            soft = jnp.maximum(z, 0.0) + jnp.log1p(e)
            sig = jnp.where(z >= 0, 1.0, e) / (1.0 + e)
            cost = weight * (soft - goal * z)
            loss = loss + jnp.sum(cost.reshape(HALF // 8, 8, ROWS), axis=0)
            coef = (scale * weight * (sig - goal)).astype(BF)
            term_p = dot(coef, emb_r[slots])
            term_r = dot(coef, emb_p[kind], TN)
            if p == 1:
                gp[kind] = term_p
            else:
                gp[kind] += term_p
            if kind == 0:
                gr[slots] = term_r
            else:
                gr[slots] += term_r

    gathers = []

    def gather(value, me, total, peer_of):
        stage = len(gathers)
        lmsg[stage] = jnp.full((8, 128), value, F32)
        lbuf[stage, me] = lmsg[stage]
        gathers.append(
            [remote(lmsg.at[stage], lbuf.at[stage, me], peer_of(k)) for k in range(1, total)]
        )

    def gathered(stage, total):
        for copy in gathers[stage]:
            copy.wait_recv()
        return jnp.sum(lbuf[stage, :total]) / 1024.0

    gr_sib = [None] * SLOTS

    def push(i):
        grsib_s[i] = gr[quarter(i, 1 - c)].astype(BF)
        gr_sib[i] = remote(grsib_s.at[i], grsib_r.at[i], SIB)

    g_opp, g_far = [], []
    push(2)
    gpsend[0] = gp[0, part(1 - h)].astype(BF)
    for k in pieces:
        g_opp.append(remote(gpsend.at[0, cut(k)], gprecv.at[0, cut(k)], NEAR))
    push(1)
    push(3)
    gpsend[1] = gp[1, part(h)].astype(BF)
    g_near = remote(gpsend.at[1], gprecv.at[1], NEAR)
    push(4)
    push(0)
    gather(jnp.sum(loss), group_id, 8, group_peer)

    def join(i):
        gr_sib[i].wait_recv()
        gr[quarter(i, c)] += grsib_r[i].astype(F32)

    def hop(i, slot, to, start=True):
        return [
            remote(grsend.at[i, cut(k)], grrecv.at[i, cut(k)], to, start) for k in pieces
        ]

    def fill(i, slot, k):
        grsend[i, cut(k)] = gr[piece(slot, c, k)].astype(BF)

    def add(slot, i, k):
        gr[piece(slot, c, k)] += grrecv[i, cut(k)].astype(F32)

    join(2)
    for k in pieces:
        fill(2, 2, k)
    home_pair = hop(2, 2, PAIR)
    join(1)
    join(3)
    home_down, home_up = hop(1, 1, DOWN, False), hop(3, 3, UP, False)

    @pl.when(odd == 0)
    def _():
        for k in pieces:
            fill(3, 3, k)
            home_up[k].start()

    @pl.when(odd == 1)
    def _():
        for k in pieces:
            fill(1, 1, k)
            home_down[k].start()

    join(4)
    join(0)
    for k in pieces:
        g_opp[k].wait_recv()
        at = rows_at((1 - h) * QUART + k * PIECE, PIECE)
        gpsend[2, cut(k)] = (gp[1, at] + gprecv[0, cut(k)].astype(F32)).astype(BF)
        g_far.append(remote(gpsend.at[2, cut(k)], gprecv.at[2, cut(k)], FAR))
        home_pair[k].wait_recv()
        add(pair_from, 2, k)

        @pl.when(odd == 0)
        def _():
            fill(1, 1, k)
            home_down[k].start()

        @pl.when(odd == 1)
        def _():
            fill(3, 3, k)
            home_up[k].start()

    gather(gathered(0, 8), y, 4, y_peer)
    home_z = hop(4, 4, BEHIND, False)
    for k in pieces:
        home_down[k].wait_recv()
        add(up_from, 1, k)
        home_up[k].wait_recv()
        add(down_from, 3, k)
        fill(4, 4, k)
        home_z[k].start()
    gather(gathered(1, 4), b // 8, 8, z_peer)

    d_far, d_sib, o_near, o_nearx = [None] * 2, [None] * 2, [None] * 2, [None] * 2

    def back(w, g):
        u = unit[w]
        inner = jnp.sum(u * g, axis=1, keepdims=True)
        d = ((g - u * inner) / norm[w, :, 0:1]).astype(BF)
        dsend[w] = d
        d_far[w] = remote(dsend.at[w], dbuf.at[w, part(c)], FAR)
        osend[w, 0] = dot(d, projs[w, 0], NT).astype(BF)
        osend[w, 1] = dot(d, projs[w, 1], NT).astype(BF)
        o_near[w] = remote(osend.at[w, 0], onear.at[w, part(c)], NEAR)
        o_nearx[w] = remote(osend.at[w, 1], onear.at[w, part(c)], NEARX)

    g_near.wait_recv()
    for link in g_far:
        link.wait_recv()
    back(1, gp[0, part(h)] + gprecv[1].astype(F32) + gprecv[2].astype(F32))

    for k in pieces:
        home_z[k].wait_recv()
        add(0, 4, k)
    back(0, gr[part(c)])
    loss_ref[0] = gathered(2, 8) / (ROWS * BLOCKS * STEPS * ROWS)

    outs = (out_r, out_p)

    def place(w, half, block):
        @pl.when(half == 0)
        def _():
            oval[w, :, :HALF] = block

        @pl.when(half == 1)
        def _():
            oval[w, :, HALF:] = block

    written = []
    d_far[1].wait_recv()
    d_sib[1] = remote(dbuf.at[1, part(c)], dbuf.at[1, part(c)], SIB)
    for w in (1, 0):
        o_near[w].wait_recv()
        o_nearx[w].wait_recv()
        place(w, h, onear[w].astype(F32).T.astype(BF))
        if w == 0:
            d_far[0].wait_recv()
            d_sib[0] = remote(dbuf.at[0, part(c)], dbuf.at[0, part(c)], SIB)
        d_sib[w].wait_recv()
        place(w, 1 - h, dot(projs[w, 0], dbuf[w], NT).astype(BF))
        written.append(load(oval.at[w], outs[w]))
    for copy in written:
        copy.wait()
    close()


def on_device(
    prompt_feats, response_feats, prompt_proj, response_proj,
    logit_scale, logit_bias, teacher, valid,
):
    anywhere = pl.BlockSpec(memory_space=pl.ANY)
    scalar = pl.BlockSpec(memory_space=pltpu.SMEM)

    def vm(*shape, kind=BF):
        return pltpu.VMEM(shape, kind)

    grad_response, grad_prompt, loss = pl.pallas_call(
        kernel,
        out_shape=(
            jax.ShapeDtypeStruct((FEAT, ROWS), BF),
            jax.ShapeDtypeStruct((FEAT, ROWS), BF),
            jax.ShapeDtypeStruct((1,), F32),
        ),
        in_specs=[anywhere] * 4 + [scalar] * 2 + [anywhere] * 2,
        out_specs=(anywhere, anywhere, scalar),
        scratch_shapes=[
            vm(2, FEAT, ROWS),
            vm(2, ROWS, FEAT),
            vm(2, 2, FEAT, EMB),
            vm(2, QUART, FEAT),
            vm(2, 2, QUART, FEAT),
            vm(2, QUART, EMB),
            vm(2, QUART, EMB),
            vm(2, QUART, EMB, kind=F32),
            vm(2, QUART, 128, kind=F32),
            vm(2, HALF, EMB),
            vm(SLOTS * HALF, EMB),
            vm(2, QUART, STEPS * ROWS, kind=jnp.int32),
            vm(2, HALF, ROWS),
            vm(2, HALF, ROWS),
            vm(2, 2, HALF, ROWS, kind=F32),
            vm(2, STEPS, ROWS, kind=jnp.int32),
            vm(2, ROWS, STEPS, kind=F32),
            vm(2, HALF, EMB, kind=F32),
            vm(SLOTS * HALF, EMB, kind=F32),
            vm(3, QUART, EMB),
            vm(3, QUART, EMB),
            vm(SLOTS, QUART, EMB),
            vm(SLOTS, QUART, EMB),
            vm(SLOTS, QUART, EMB),
            vm(SLOTS, QUART, EMB),
            vm(2, QUART, EMB),
            vm(2, HALF, EMB),
            vm(2, 2, QUART, FEAT),
            vm(2, HALF, FEAT),
            vm(2, FEAT, ROWS),
            vm(3, 8, 128, kind=F32),
            vm(3, 8, 8, 128, kind=F32),
            pltpu.SemaphoreType.DMA((104,)),
            pltpu.SemaphoreType.DMA((104,)),
            pltpu.SemaphoreType.DMA((16,)),
        ],
        compiler_params=pltpu.CompilerParams(
            collective_id=0, has_side_effects=True, vmem_limit_bytes=56 * 2**20
        ),
        name="band",
    )(
        response_feats.T, prompt_feats.T, response_proj, prompt_proj,
        logit_scale, logit_bias, teacher, valid.T,
    )
    return grad_prompt.T, grad_response.T, loss


def solution(mesh):
    in_specs = (
        P("batch", "tower"), P("batch", "tower"), P("tower", None), P("tower", None),
        P(), P(), P("batch", None), P("batch", None),
    )
    out_specs = (P("batch", "tower"), P("batch", "tower"), P())
    return jax.shard_map(
        on_device, mesh=mesh, in_specs=in_specs, out_specs=out_specs, check_vma=False
    )
```

time: 97.8 us -> 83.3 us (0.85); the launches traced: 96.7 us -> 83.2 us
  Pallas kernels: 84.2 us -> 76.1 us
  local copies, waits for them, and re-layouts: 8.73 us -> 3.29 us
    pallas_call x1, Pallas kernels: 84.2 us -> 76.1 us  [on_device(): pl.pallas_call(kernel, out_shape=(jax.ShapeDtypeStruct((FEAT, ROWS), BF),...]
    unnamed x5 -> x2, local copies, waits for them, and re-layouts: 8.73 us -> 3.29 us
where the time goes in v2:
time: 83.3 us; the launch traced here: 83.2 us
  Pallas kernels  76.1 us (91%)
  between operations  3.75 us (5%)
  local copies, waits for them, and re-layouts  3.29 us (4%)
    pallas_call x1, Pallas kernels, on_device(): pl.pallas_call(kernel, out_shape=(jax.ShapeDtypeStruct((FEAT, ROWS), BF),...  76.1 us
    unnamed x2, local copies, waits for them, and re-layouts  3.29 us

profile of v2, /device:TPU:1, one launch (start us, length us, event | category | flops | bytes accessed | tf_op | source)
XLA Modules:
  0.0 83.2 jit_solution(13907093021265511023)
XLA Ops:
  1.9 76.1 %band.1 = (bf16[288,384]{1,0:T(8,128)(2,1)}, bf16[288,384]{1,0:T(8,128)(2,1)}, f32[1]{0:T(128)}) custom-call(bf16[288,384]{1,0:T(8,128)(2,1)} %bitcast.7, bf16[288,384]{1,0:T(8,128)(2,1)} %bitcast.8, bf16[288,1152]{1,0:T(8,128)(2,1)} %proj_r.1, bf16[288,1152]{1,0:T(8,128)(2,1)} %proj_p.1, f32[1]{0:T(128)S(6)} %copy.14.scale_ref, f32[1]{0:T(128)S(6)} %copy.15.bias_ref, ...), custom_call_target="tpu_custom_call" | custom-call | tf_op jit(solution)/shard_map/band/pallas_call | solution.py:491
  78.1 1.6 %copy.16 = bf16[384,288]{0,1:T(8,128)(2,1)} copy(bf16[384,288]{0,1:T(8,128)(2,1)} %bitcast.6) | data formatting | bytes 442368
  79.7 1.6 %copy.17 = bf16[384,288]{0,1:T(8,128)(2,1)} copy(bf16[384,288]{0,1:T(8,128)(2,1)} %bitcast.5) | data formatting | bytes 442368

commit v3 on v2

--- a/solution.py
+++ b/solution.py
@@ -8,7 +8,7 @@
 BF, F32 = jnp.bfloat16, jnp.float32
 ROWS, FEAT, EMB, STEPS, BLOCKS, TOWER = 384, 288, 1152, 8, 64, 4
 HALF, QUART = ROWS // 2, ROWS // 4
-SLOTS, PIECE = 5, 48
+SLOTS, PIECE = 5, 32
 NT = (((1,), (1,)), ((), ()))
 TN = (((0,), (0,)), ((), ()))
 
@@ -25,8 +25,8 @@
 def kernel(
     feats_r, feats_p, proj_r, proj_p, scale_ref, bias_ref, teach, valid,
     out_r, out_p, loss_ref,
-    fcols, frows, projs, feat_f, feat_n, fsend, frecv, unit, norm, emb_p, emb_r,
-    traw, tsend, trecv, target, vcols, vrows, gp, gr, gpsend, gprecv,
+    fcols, frows, projs, part_sum, sib_send, sib_recv, feat_n, fsend, frecv, unit, norm, emb_p, emb_r,
+    traw, tsend, trecv, target, vcols, vrows, coefs, gp, gr, gpsend, gprecv,
     grsib_s, grsib_r, grsend, grrecv, dsend, dbuf, osend, onear, oval,
     lmsg, lbuf, send_sem, recv_sem, loc_sem,
 ):
@@ -128,39 +128,33 @@
     own_teach = [load(teach.at[quarter(hh, c)], traw.at[hh]) for hh in (0, 1)]
     own_valid = load(valid, vcols.at[1])
 
+    def own_sum(w):
+        own_proj[w].wait()
+        part_sum[w] = dot(frows[w, rows_at((1 - h) * HALF, HALF)], projs[w, 0])
+        sib_send[w] = part_sum[w, part(1 - c)].astype(BF)
+
     for w in (0, 1):
         own_feat[w].wait()
         frows[w] = fcols[w].astype(F32).T.astype(BF)
+        if w == 0:
+            own_sum(0)
     pl.semaphore_wait(barrier, len(peers))
 
-    to_sib, feat_sib, feat_near, feat_nearx = [], [], [], []
+    sum_sib, to_sib, feat_near, feat_nearx, partial = [], [], [], [], []
 
     def enter(w):
-        feat_sib.append(remote(frows.at[w, quarter(1 - h, 1 - c)], feat_f.at[w], SIB))
-        to_sib.append(remote(proj[w], projs.at[w, 1], SIB))
+        sum_sib.append(remote(sib_send.at[w], sib_recv.at[w], SIB))
         feat_near.append(remote(frows.at[w, quarter(h, c)], feat_n.at[w, 0], NEAR))
         feat_nearx.append(remote(frows.at[w, quarter(h, 1 - c)], feat_n.at[w, 1], NEARX))
 
-    partial = []
-
-    def half_sum(w):
-        own_proj[w].wait()
-        acc = dot(frows[w, quarter(1 - h, c)], projs[w, 0])
-        feat_sib[w].wait_recv()
-        to_sib[w].wait_recv()
-        acc += dot(feat_f[w], projs[w, 1])
-        fsend[w] = acc.astype(BF)
+    enter(0)
+    own_sum(1)
+    enter(1)
+    for w in (0, 1):
+        sum_sib[w].wait_recv()
+        fsend[w] = (part_sum[w, part(c)] + sib_recv[w].astype(F32)).astype(BF)
         partial.append(remote(fsend.at[w], frecv.at[w], FAR))
-
-    enter(0)
-    own_proj[0].wait()
-    first = dot(frows[0, quarter(1 - h, c)], projs[0, 0])
-    feat_sib[0].wait_recv()
-    to_sib[0].wait_recv()
-    enter(1)
-    fsend[0] = (first + dot(feat_f[0], projs[0, 1])).astype(BF)
-    partial.append(remote(fsend.at[0], frecv.at[0], FAR))
-    half_sum(1)
+        to_sib.append(remote(proj[w], projs.at[w, 1], SIB))
 
     for copy in own_teach:
         copy.wait()
@@ -185,6 +179,7 @@
     gr[4 * HALF:] = jnp.zeros((HALF, EMB), F32)
 
     def finish(w):
+        to_sib[w].wait_recv()
         feat_near[w].wait_recv()
         feat_nearx[w].wait_recv()
         pre = dot(feat_n[w, 0], projs[w, 0]) + dot(feat_n[w, 1], projs[w, 1])
@@ -227,25 +222,26 @@
     resp_sib = [None] * SLOTS
     resp_sib[0] = resp_over(0)
 
-    fresh = finish(1)
-    emb_p[0, part(h)] = fresh
+    def zrelay(k):
+        zhop[k].wait_recv()
+
+        @pl.when(y == 3)
+        def _():
+            up[k].start()
+
+        @pl.when(y > 0)
+        def _():
+            down[k].start()
+
+    zrelay(0)
+    emb_p[0, part(h)] = finish(1)
     p_far, p_near, p_opp = [], [], []
     for k in pieces:
         at = rows_at(h * QUART + k * PIECE, PIECE)
         p_far.append(remote(emb_p.at[0, at], emb_p.at[1, at], FAR))
         p_near.append(remote(emb_p.at[0, at], emb_p.at[1, at], NEAR))
-
-    for k in pieces:
-        zhop[k].wait_recv()
-
-        @pl.when(y == 3)
-        def _():
-            up[k].start()
-
-        @pl.when(y > 0)
-        def _():
-            down[k].start()
-
+    for k in pieces[1:]:
+        zrelay(k)
     resp_sib[4] = resp_over(4)
 
     teach_near.wait_recv()
@@ -291,9 +287,13 @@
 
     scale, bias = scale_ref[0], bias_ref[0]
     loss = jnp.zeros((8, ROWS), F32)
+
+    def met(kind, p):
+        return pl.ds(pl.multiple_of((2 * p + kind * (1 - l)) * HALF, 64), ROWS)
+
     for p in (1, 0):
         for kind in (0, 1):
-            slots = pl.ds(pl.multiple_of((2 * p + kind * (1 - l)) * HALF, 64), ROWS)
+            slots = met(kind, p)
             step = 4 * p + kind
             weight = jnp.concatenate(
                 [
@@ -314,12 +314,8 @@
             cost = weight * (soft - goal * z)
             loss = loss + jnp.sum(cost.reshape(HALF // 8, 8, ROWS), axis=0)
             coef = (scale * weight * (sig - goal)).astype(BF)
-            term_p = dot(coef, emb_r[slots])
+            coefs[kind, p] = coef
             term_r = dot(coef, emb_p[kind], TN)
-            if p == 1:
-                gp[kind] = term_p
-            else:
-                gp[kind] += term_p
             if kind == 0:
                 gr[slots] = term_r
             else:
@@ -329,8 +325,8 @@
 
     def gather(value, me, total, peer_of):
         stage = len(gathers)
-        lmsg[stage] = jnp.full((8, 128), value, F32)
-        lbuf[stage, me] = lmsg[stage]
+        lmsg[stage] = value
+        lbuf[stage, me] = value
         gathers.append(
             [remote(lmsg.at[stage], lbuf.at[stage, me], peer_of(k)) for k in range(1, total)]
         )
@@ -338,7 +334,7 @@
     def gathered(stage, total):
         for copy in gathers[stage]:
             copy.wait_recv()
-        return jnp.sum(lbuf[stage, :total]) / 1024.0
+        return jnp.sum(lbuf[stage, :total], axis=0)
 
     gr_sib = [None] * SLOTS
 
@@ -346,108 +342,117 @@
         grsib_s[i] = gr[quarter(i, 1 - c)].astype(BF)
         gr_sib[i] = remote(grsib_s.at[i], grsib_r.at[i], SIB)
 
-    g_opp, g_far = [], []
-    push(2)
-    gpsend[0] = gp[0, part(1 - h)].astype(BF)
-    for k in pieces:
-        g_opp.append(remote(gpsend.at[0, cut(k)], gprecv.at[0, cut(k)], NEAR))
-    push(1)
-    push(3)
-    gpsend[1] = gp[1, part(h)].astype(BF)
-    g_near = remote(gpsend.at[1], gprecv.at[1], NEAR)
-    push(4)
-    push(0)
-    gather(jnp.sum(loss), group_id, 8, group_peer)
-
     def join(i):
         gr_sib[i].wait_recv()
         gr[quarter(i, c)] += grsib_r[i].astype(F32)
 
-    def hop(i, slot, to, start=True):
+    def hop(i, to):
         return [
-            remote(grsend.at[i, cut(k)], grrecv.at[i, cut(k)], to, start) for k in pieces
+            remote(grsend.at[i, cut(k)], grrecv.at[i, cut(k)], to, False) for k in pieces
         ]
 
-    def fill(i, slot, k):
-        grsend[i, cut(k)] = gr[piece(slot, c, k)].astype(BF)
+    def fill(i, k):
+        grsend[i, cut(k)] = gr[piece(i, c, k)].astype(BF)
 
     def add(slot, i, k):
         gr[piece(slot, c, k)] += grrecv[i, cut(k)].astype(F32)
 
+    for i in (2, 1, 3, 4, 0):
+        push(i)
+    for kind in (0, 1):
+        gp[kind] = dot(coefs[kind, 0], emb_r[met(kind, 0)]) + dot(coefs[kind, 1], emb_r[met(kind, 1)])
+        if kind == 0:
+            gpsend[0] = gp[0, part(1 - h)].astype(BF)
+            g_opp = [
+                remote(gpsend.at[0, cut(k)], gprecv.at[0, cut(k)], NEAR) for k in pieces
+            ]
+    home_pair, home_down, home_up, home_z = hop(2, PAIR), hop(1, DOWN), hop(3, UP), hop(4, BEHIND)
     join(2)
     for k in pieces:
-        fill(2, 2, k)
-    home_pair = hop(2, 2, PAIR)
+        fill(2, k)
+        home_pair[k].start()
     join(1)
     join(3)
-    home_down, home_up = hop(1, 1, DOWN, False), hop(3, 3, UP, False)
 
     @pl.when(odd == 0)
     def _():
         for k in pieces:
-            fill(3, 3, k)
+            fill(3, k)
             home_up[k].start()
 
     @pl.when(odd == 1)
     def _():
         for k in pieces:
-            fill(1, 1, k)
+            fill(1, k)
             home_down[k].start()
 
+    lanes = [loss[:, 128 * i:128 * (i + 1)] for i in range(ROWS // 128)]
+    gather(lanes[0] + lanes[1] + lanes[2], group_id, 8, group_peer)
+    gpsend[1] = gp[1, part(h)].astype(BF)
     join(4)
     join(0)
-    for k in pieces:
+    g_far, g_near = [], []
+    for k in pieces:
+        home_pair[k].wait_recv()
+        add(pair_from, 2, k)
+
+        @pl.when(odd == 0)
+        def _():
+            fill(1, k)
+            home_down[k].start()
+
+        @pl.when(odd == 1)
+        def _():
+            fill(3, k)
+            home_up[k].start()
+
         g_opp[k].wait_recv()
         at = rows_at((1 - h) * QUART + k * PIECE, PIECE)
         gpsend[2, cut(k)] = (gp[1, at] + gprecv[0, cut(k)].astype(F32)).astype(BF)
         g_far.append(remote(gpsend.at[2, cut(k)], gprecv.at[2, cut(k)], FAR))
-        home_pair[k].wait_recv()
-        add(pair_from, 2, k)
-
-        @pl.when(odd == 0)
-        def _():
-            fill(1, 1, k)
-            home_down[k].start()
-
-        @pl.when(odd == 1)
-        def _():
-            fill(3, 3, k)
-            home_up[k].start()
+        g_near.append(remote(gpsend.at[1, cut(k)], gprecv.at[1, cut(k)], NEAR))
 
     gather(gathered(0, 8), y, 4, y_peer)
-    home_z = hop(4, 4, BEHIND, False)
+
+    d_far, d_sib, o_near, o_nearx = [[], []], [[], []], [None] * 2, [None] * 2
+
+    def back(w, k, g):
+        u = unit[w, cut(k)]
+        inner = jnp.sum(u * g, axis=1, keepdims=True)
+        dsend[w, cut(k)] = ((g - u * inner) / norm[w, cut(k), 0:1]).astype(BF)
+        d_far[w].append(remote(dsend.at[w, cut(k)], dbuf.at[w, piece(0, c, k)], FAR))
+
+    def product(w):
+        d = dsend[w]
+        osend[w, 0] = dot(d, projs[w, 0], NT).astype(BF)
+        osend[w, 1] = dot(d, projs[w, 1], NT).astype(BF)
+        o_near[w] = remote(osend.at[w, 0], onear.at[w, part(c)], NEAR)
+        o_nearx[w] = remote(osend.at[w, 1], onear.at[w, part(c)], NEARX)
+
+    def forward(w):
+        for k in pieces:
+            d_far[w][k].wait_recv()
+            at = piece(0, c, k)
+            d_sib[w].append(remote(dbuf.at[w, at], dbuf.at[w, at], SIB))
+
     for k in pieces:
         home_down[k].wait_recv()
         add(up_from, 1, k)
         home_up[k].wait_recv()
         add(down_from, 3, k)
-        fill(4, 4, k)
+        fill(4, k)
         home_z[k].start()
+        g_near[k].wait_recv()
+        g_far[k].wait_recv()
+        at = rows_at(h * QUART + k * PIECE, PIECE)
+        back(1, k, gp[0, at] + gprecv[1, cut(k)].astype(F32) + gprecv[2, cut(k)].astype(F32))
     gather(gathered(1, 4), b // 8, 8, z_peer)
-
-    d_far, d_sib, o_near, o_nearx = [None] * 2, [None] * 2, [None] * 2, [None] * 2
-
-    def back(w, g):
-        u = unit[w]
-        inner = jnp.sum(u * g, axis=1, keepdims=True)
-        d = ((g - u * inner) / norm[w, :, 0:1]).astype(BF)
-        dsend[w] = d
-        d_far[w] = remote(dsend.at[w], dbuf.at[w, part(c)], FAR)
-        osend[w, 0] = dot(d, projs[w, 0], NT).astype(BF)
-        osend[w, 1] = dot(d, projs[w, 1], NT).astype(BF)
-        o_near[w] = remote(osend.at[w, 0], onear.at[w, part(c)], NEAR)
-        o_nearx[w] = remote(osend.at[w, 1], onear.at[w, part(c)], NEARX)
-
-    g_near.wait_recv()
-    for link in g_far:
-        link.wait_recv()
-    back(1, gp[0, part(h)] + gprecv[1].astype(F32) + gprecv[2].astype(F32))
-
     for k in pieces:
         home_z[k].wait_recv()
-        add(0, 4, k)
-    back(0, gr[part(c)])
-    loss_ref[0] = gathered(2, 8) / (ROWS * BLOCKS * STEPS * ROWS)
+        back(0, k, gr[piece(0, c, k)] + grrecv[4, cut(k)].astype(F32))
+    product(1)
+    product(0)
+    forward(1)
 
     outs = (out_r, out_p)
 
@@ -461,18 +466,17 @@
             oval[w, :, HALF:] = block
 
     written = []
-    d_far[1].wait_recv()
-    d_sib[1] = remote(dbuf.at[1, part(c)], dbuf.at[1, part(c)], SIB)
     for w in (1, 0):
+        if w == 0:
+            forward(0)
         o_near[w].wait_recv()
         o_nearx[w].wait_recv()
         place(w, h, onear[w].astype(F32).T.astype(BF))
-        if w == 0:
-            d_far[0].wait_recv()
-            d_sib[0] = remote(dbuf.at[0, part(c)], dbuf.at[0, part(c)], SIB)
-        d_sib[w].wait_recv()
+        for link in d_sib[w]:
+            link.wait_recv()
         place(w, 1 - h, dot(projs[w, 0], dbuf[w], NT).astype(BF))
         written.append(load(oval.at[w], outs[w]))
+    loss_ref[0] = jnp.sum(gathered(2, 8)) / (ROWS * BLOCKS * STEPS * ROWS)
     for copy in written:
         copy.wait()
     close()
@@ -501,7 +505,9 @@
             vm(2, FEAT, ROWS),
             vm(2, ROWS, FEAT),
             vm(2, 2, FEAT, EMB),
-            vm(2, QUART, FEAT),
+            vm(2, HALF, EMB, kind=F32),
+            vm(2, QUART, EMB),
+            vm(2, QUART, EMB),
             vm(2, 2, QUART, FEAT),
             vm(2, QUART, EMB),
             vm(2, QUART, EMB),
@@ -515,6 +521,7 @@
             vm(2, 2, HALF, ROWS, kind=F32),
             vm(2, STEPS, ROWS, kind=jnp.int32),
             vm(2, ROWS, STEPS, kind=F32),
+            vm(2, 2, HALF, ROWS),
             vm(2, HALF, EMB, kind=F32),
             vm(SLOTS * HALF, EMB, kind=F32),
             vm(3, QUART, EMB),
@@ -530,8 +537,8 @@
             vm(2, FEAT, ROWS),
             vm(3, 8, 128, kind=F32),
             vm(3, 8, 8, 128, kind=F32),
-            pltpu.SemaphoreType.DMA((104,)),
-            pltpu.SemaphoreType.DMA((104,)),
+            pltpu.SemaphoreType.DMA((112,)),
+            pltpu.SemaphoreType.DMA((112,)),
             pltpu.SemaphoreType.DMA((16,)),
         ],
         compiler_params=pltpu.CompilerParams(

time: 83.3 us -> 74.6 us (0.90)
  Pallas kernels: 76.1 us -> 67.4 us
    pallas_call x1, Pallas kernels: 76.1 us -> 67.4 us  [on_device(): pl.pallas_call(kernel, out_shape=(jax.ShapeDtypeStruct((FEAT, ROWS), BF),...]
where the time goes in v3:
time: 74.6 us; the launch traced here: 74.4 us
  Pallas kernels  67.4 us (90%)
  between operations  3.75 us (5%)
  local copies, waits for them, and re-layouts  3.29 us (4%)
    pallas_call x1, Pallas kernels, on_device(): pl.pallas_call(kernel, out_shape=(jax.ShapeDtypeStruct((FEAT, ROWS), BF),...  67.4 us
    unnamed x2, local copies, waits for them, and re-layouts  3.29 us

profile of v3, /device:TPU:1, one launch (start us, length us, event | category | flops | bytes accessed | tf_op | source)
XLA Modules:
  0.0 74.4 jit_solution(18145844147151643070)
XLA Ops:
  1.9 67.4 %band.1 = (bf16[288,384]{1,0:T(8,128)(2,1)}, bf16[288,384]{1,0:T(8,128)(2,1)}, f32[1]{0:T(128)}) custom-call(bf16[288,384]{1,0:T(8,128)(2,1)} %bitcast.7, bf16[288,384]{1,0:T(8,128)(2,1)} %bitcast.8, bf16[288,1152]{1,0:T(8,128)(2,1)} %proj_r.1, bf16[288,1152]{1,0:T(8,128)(2,1)} %proj_p.1, f32[1]{0:T(128)S(6)} %copy.14.scale_ref, f32[1]{0:T(128)S(6)} %copy.15.bias_ref, ...), custom_call_target="tpu_custom_call" | custom-call | tf_op jit(solution)/shard_map/band/pallas_call | solution.py:495
  69.3 1.6 %copy.16 = bf16[384,288]{0,1:T(8,128)(2,1)} copy(bf16[384,288]{0,1:T(8,128)(2,1)} %bitcast.6) | data formatting | bytes 442368
  71.0 1.6 %copy.17 = bf16[384,288]{0,1:T(8,128)(2,1)} copy(bf16[384,288]{0,1:T(8,128)(2,1)} %bitcast.5) | data formatting | bytes 442368

commit v4 on v3

--- a/solution.py
+++ b/solution.py
@@ -24,10 +24,10 @@
 
 def kernel(
     feats_r, feats_p, proj_r, proj_p, scale_ref, bias_ref, teach, valid,
-    out_r, out_p, loss_ref,
+    oval, loss_ref,
     fcols, frows, projs, part_sum, sib_send, sib_recv, feat_n, fsend, frecv, unit, norm, emb_p, emb_r,
     traw, tsend, trecv, target, vcols, vrows, coefs, gp, gr, gpsend, gprecv,
-    grsib_s, grsib_r, grsend, grrecv, dsend, dbuf, osend, onear, oval,
+    grsib_s, grsib_r, grsend, grrecv, dsend, dbuf, osend, onear,
     lmsg, lbuf, send_sem, recv_sem, loc_sem,
 ):
     b = lax.axis_index("batch")
@@ -150,10 +150,13 @@
     enter(0)
     own_sum(1)
     enter(1)
+    pieces = range(QUART // PIECE)
     for w in (0, 1):
         sum_sib[w].wait_recv()
         fsend[w] = (part_sum[w, part(c)] + sib_recv[w].astype(F32)).astype(BF)
-        partial.append(remote(fsend.at[w], frecv.at[w], FAR))
+        partial.append(
+            [remote(fsend.at[w, cut(k)], frecv.at[w, cut(k)], FAR, w == 0) for k in pieces]
+        )
         to_sib.append(remote(proj[w], projs.at[w, 1], SIB))
 
     for copy in own_teach:
@@ -178,25 +181,25 @@
             target[1, p, hh * QUART:(hh + 1) * QUART] = sigmoid(steps_of(hh, 4 * p + 1) / 32.0)
     gr[4 * HALF:] = jnp.zeros((HALF, EMB), F32)
 
-    def finish(w):
+    def near_sum(w):
         to_sib[w].wait_recv()
         feat_near[w].wait_recv()
         feat_nearx[w].wait_recv()
-        pre = dot(feat_n[w, 0], projs[w, 0]) + dot(feat_n[w, 1], projs[w, 1])
-        partial[w].wait_recv()
-        pre = pre + frecv[w].astype(F32)
+        unit[w] = dot(feat_n[w, 0], projs[w, 0]) + dot(feat_n[w, 1], projs[w, 1])
+
+    def finish(w, k):
+        pre = unit[w, cut(k)] + frecv[w, cut(k)].astype(F32)
         length = jnp.sqrt(jnp.sum(pre * pre, axis=1, keepdims=True) + 1e-06)
-        norm[w] = jnp.broadcast_to(length, (QUART, 128))
+        norm[w, cut(k)] = jnp.broadcast_to(length, (PIECE, 128))
         u = pre / length
-        unit[w] = u
+        unit[w, cut(k)] = u
         return u.astype(BF)
 
-    pieces = range(ROWS // 4 // PIECE)
     up_from, down_from, pair_from = (y // 3) * 4, ((y + 3) // 4) * 4, 1 + 2 * odd
 
-    def relay(src, dst, to, start=True):
+    def relay(src, dst, to):
         return [
-            remote(emb_r.at[piece(src, c, k)], emb_r.at[piece(dst, c, k)], to, start)
+            remote(emb_r.at[piece(src, c, k)], emb_r.at[piece(dst, c, k)], to, False)
             for k in pieces
         ]
 
@@ -204,20 +207,23 @@
         at = quarter(slot, c)
         return remote(emb_r.at[at], emb_r.at[at], SIB)
 
-    emb_r[part(c)] = finish(0)
     zhop = relay(0, 4, AHEAD)
-    up, down = relay(up_from, 1, UP, False), relay(down_from, 3, DOWN, False)
-    pair = relay(pair_from, 2, PAIR, False)
-
-    @pl.when(y < 3)
-    def _():
-        for link in up:
-            link.start()
-
-    @pl.when(y == 0)
-    def _():
-        for link in down:
-            link.start()
+    up, down = relay(up_from, 1, UP), relay(down_from, 3, DOWN)
+    pair = relay(pair_from, 2, PAIR)
+    near_sum(0)
+    for k in pieces:
+        partial[0][k].wait_recv()
+        partial[1][k].start()
+        emb_r[piece(0, c, k)] = finish(0, k)
+        zhop[k].start()
+
+        @pl.when(y < 3)
+        def _():
+            up[k].start()
+
+        @pl.when(y == 0)
+        def _():
+            down[k].start()
 
     resp_sib = [None] * SLOTS
     resp_sib[0] = resp_over(0)
@@ -233,15 +239,15 @@
         def _():
             down[k].start()
 
-    zrelay(0)
-    emb_p[0, part(h)] = finish(1)
+    near_sum(1)
     p_far, p_near, p_opp = [], [], []
     for k in pieces:
+        zrelay(k)
+        partial[1][k].wait_recv()
         at = rows_at(h * QUART + k * PIECE, PIECE)
+        emb_p[0, at] = finish(1, k)
         p_far.append(remote(emb_p.at[0, at], emb_p.at[1, at], FAR))
         p_near.append(remote(emb_p.at[0, at], emb_p.at[1, at], NEAR))
-    for k in pieces[1:]:
-        zrelay(k)
     resp_sib[4] = resp_over(4)
 
     teach_near.wait_recv()
@@ -285,26 +291,57 @@
     for i in (4, 3, 2, 1, 0):
         resp_sib[i].wait_recv()
 
+    def push(i):
+        grsib_s[i] = gr[quarter(i, 1 - c)].astype(BF)
+        return remote(grsib_s.at[i], grsib_r.at[i], SIB)
+
+    def join(i, link):
+        link.wait_recv()
+        gr[quarter(i, c)] += grsib_r[i].astype(F32)
+
+    def hop(i, to):
+        return [
+            remote(grsend.at[i, cut(k)], grrecv.at[i, cut(k)], to, False) for k in pieces
+        ]
+
+    def fill(i, k):
+        grsend[i, cut(k)] = gr[piece(i, c, k)].astype(BF)
+
+    def add(slot, i, k):
+        gr[piece(slot, c, k)] += grrecv[i, cut(k)].astype(F32)
+
+    home_pair, home_down, home_up, home_z = hop(2, PAIR), hop(1, DOWN), hop(3, UP), hop(4, BEHIND)
+
+    def send_soon():
+        @pl.when(odd == 0)
+        def _():
+            for k in pieces:
+                fill(3, k)
+                home_up[k].start()
+
+        @pl.when(odd == 1)
+        def _():
+            for k in pieces:
+                fill(1, k)
+                home_down[k].start()
+
     scale, bias = scale_ref[0], bias_ref[0]
     loss = jnp.zeros((8, ROWS), F32)
 
     def met(kind, p):
         return pl.ds(pl.multiple_of((2 * p + kind * (1 - l)) * HALF, 64), ROWS)
 
+    soon = 4 - pair_from
     for p in (1, 0):
         for kind in (0, 1):
             slots = met(kind, p)
-            step = 4 * p + kind
+
+            def column(hh, s):
+                at = 4 * p + s
+                return vrows[kind, quarter(hh, c), at:at + 1]
+
             weight = jnp.concatenate(
-                [
-                    jnp.where(
-                        early,
-                        vrows[kind, quarter(hh, c), step:step + 1],
-                        vrows[kind, quarter(hh, c), step + 2:step + 3],
-                    )
-                    for hh in (0, 1)
-                ],
-                axis=0,
+                [jnp.where(early, column(hh, kind), column(hh, kind + 2)) for hh in (0, 1)], axis=0
             )
             goal = target[kind, p]
             z = scale * dot(emb_p[kind], emb_r[slots], NT) + bias
@@ -336,29 +373,7 @@
             copy.wait_recv()
         return jnp.sum(lbuf[stage, :total], axis=0)
 
-    gr_sib = [None] * SLOTS
-
-    def push(i):
-        grsib_s[i] = gr[quarter(i, 1 - c)].astype(BF)
-        gr_sib[i] = remote(grsib_s.at[i], grsib_r.at[i], SIB)
-
-    def join(i):
-        gr_sib[i].wait_recv()
-        gr[quarter(i, c)] += grsib_r[i].astype(F32)
-
-    def hop(i, to):
-        return [
-            remote(grsend.at[i, cut(k)], grrecv.at[i, cut(k)], to, False) for k in pieces
-        ]
-
-    def fill(i, k):
-        grsend[i, cut(k)] = gr[piece(i, c, k)].astype(BF)
-
-    def add(slot, i, k):
-        gr[piece(slot, c, k)] += grrecv[i, cut(k)].astype(F32)
-
-    for i in (2, 1, 3, 4, 0):
-        push(i)
+    sib_pair, sib_soon, sib_late, sib_four, sib_zero = [push(i) for i in (2, soon, pair_from, 4, 0)]
     for kind in (0, 1):
         gp[kind] = dot(coefs[kind, 0], emb_r[met(kind, 0)]) + dot(coefs[kind, 1], emb_r[met(kind, 1)])
         if kind == 0:
@@ -366,31 +381,18 @@
             g_opp = [
                 remote(gpsend.at[0, cut(k)], gprecv.at[0, cut(k)], NEAR) for k in pieces
             ]
-    home_pair, home_down, home_up, home_z = hop(2, PAIR), hop(1, DOWN), hop(3, UP), hop(4, BEHIND)
-    join(2)
+    join(2, sib_pair)
     for k in pieces:
         fill(2, k)
         home_pair[k].start()
-    join(1)
-    join(3)
-
-    @pl.when(odd == 0)
-    def _():
-        for k in pieces:
-            fill(3, k)
-            home_up[k].start()
-
-    @pl.when(odd == 1)
-    def _():
-        for k in pieces:
-            fill(1, k)
-            home_down[k].start()
-
+    join(soon, sib_soon)
+    send_soon()
+    join(pair_from, sib_late)
     lanes = [loss[:, 128 * i:128 * (i + 1)] for i in range(ROWS // 128)]
     gather(lanes[0] + lanes[1] + lanes[2], group_id, 8, group_peer)
     gpsend[1] = gp[1, part(h)].astype(BF)
-    join(4)
-    join(0)
+    join(4, sib_four)
+    join(0, sib_zero)
     g_far, g_near = [], []
     for k in pieces:
         home_pair[k].wait_recv()
@@ -454,8 +456,6 @@
     product(0)
     forward(1)
 
-    outs = (out_r, out_p)
-
     def place(w, half, block):
         @pl.when(half == 0)
         def _():
@@ -465,7 +465,6 @@
         def _():
             oval[w, :, HALF:] = block
 
-    written = []
     for w in (1, 0):
         if w == 0:
             forward(0)
@@ -475,11 +474,16 @@
         for link in d_sib[w]:
             link.wait_recv()
         place(w, 1 - h, dot(projs[w, 0], dbuf[w], NT).astype(BF))
-        written.append(load(oval.at[w], outs[w]))
     loss_ref[0] = jnp.sum(gathered(2, 8)) / (ROWS * BLOCKS * STEPS * ROWS)
-    for copy in written:
+    close()
+
+
+def deliver(grads, out_r, out_p, sem):
+    copies = [pltpu.make_async_copy(grads.at[w], (out_r, out_p)[w], sem.at[w]) for w in (0, 1)]
+    for copy in copies:
+        copy.start()
+    for copy in copies:
         copy.wait()
-    close()
 
 
 def on_device(
@@ -492,15 +496,14 @@
     def vm(*shape, kind=BF):
         return pltpu.VMEM(shape, kind)
 
-    grad_response, grad_prompt, loss = pl.pallas_call(
+    grads, loss = pl.pallas_call(
         kernel,
         out_shape=(
-            jax.ShapeDtypeStruct((FEAT, ROWS), BF),
-            jax.ShapeDtypeStruct((FEAT, ROWS), BF),
+            pltpu.VMEM((2, FEAT, ROWS), BF),
             jax.ShapeDtypeStruct((1,), F32),
         ),
         in_specs=[anywhere] * 4 + [scalar] * 2 + [anywhere] * 2,
-        out_specs=(anywhere, anywhere, scalar),
+        out_specs=(pl.BlockSpec(memory_space=pltpu.VMEM), scalar),
         scratch_shapes=[
             vm(2, FEAT, ROWS),
             vm(2, ROWS, FEAT),
@@ -534,11 +537,10 @@
             vm(2, HALF, EMB),
             vm(2, 2, QUART, FEAT),
             vm(2, HALF, FEAT),
-            vm(2, FEAT, ROWS),
             vm(3, 8, 128, kind=F32),
             vm(3, 8, 8, 128, kind=F32),
-            pltpu.SemaphoreType.DMA((112,)),
-            pltpu.SemaphoreType.DMA((112,)),
+            pltpu.SemaphoreType.DMA((128,)),
+            pltpu.SemaphoreType.DMA((128,)),
             pltpu.SemaphoreType.DMA((16,)),
         ],
         compiler_params=pltpu.CompilerParams(
@@ -549,6 +551,14 @@
         response_feats.T, prompt_feats.T, response_proj, prompt_proj,
         logit_scale, logit_bias, teacher, valid.T,
     )
+    grad_response, grad_prompt = pl.pallas_call(
+        deliver,
+        out_shape=(jax.ShapeDtypeStruct((FEAT, ROWS), BF),) * 2,
+        in_specs=[pl.BlockSpec(memory_space=pltpu.VMEM)],
+        out_specs=(anywhere, anywhere),
+        scratch_shapes=[pltpu.SemaphoreType.DMA((2,))],
+        name="deliver",
+    )(pltpu.with_memory_space_constraint(grads, pltpu.VMEM))
     return grad_prompt.T, grad_response.T, loss
 
 

time: 74.6 us -> 69.6 us (0.933)
  local copies, waits for them, and re-layouts: 3.29 us -> 0 us
  Pallas kernels: 67.4 us -> 65.8 us
    unnamed x2 -> x0, local copies, waits for them, and re-layouts: 3.29 us -> none
    pallas_call x1 -> x2, Pallas kernels: 67.4 us -> 65.8 us  [the longest x1 65 us: on_device(): pl.pallas_call(kernel, out_shape=(pltpu.VMEM((2, FEAT, ROWS), BF), jax.Sh...]
where the time goes in v4:
time: 69.6 us; the launch traced here: 69.5 us
  Pallas kernels  65.8 us (95%)
  between operations  3.7 us (5%)
    pallas_call x1, Pallas kernels, on_device(): pl.pallas_call(kernel, out_shape=(pltpu.VMEM((2, FEAT, ROWS), BF), jax.Sh...  65 us

profile of v4, /device:TPU:1, one launch (start us, length us, event | category | flops | bytes accessed | tf_op | source)
XLA Modules:
  0.0 69.5 jit_solution(2610762635762216872)
XLA Ops:
  1.9 65.0 %band.1 = (bf16[2,288,384]{2,1,0:T(8,128)(2,1)S(1)}, f32[1]{0:T(128)}) custom-call(bf16[288,384]{1,0:T(8,128)(2,1)} %bitcast.5, bf16[288,384]{1,0:T(8,128)(2,1)} %bitcast.6, bf16[288,1152]{1,0:T(8,128)(2,1)} %proj_r.1, bf16[288,1152]{1,0:T(8,128)(2,1)} %proj_p.1, f32[1]{0:T(128)S(6)} %copy.12.scale_ref, f32[1]{0:T(128)S(6)} %copy.13.bias_ref, ...), custom_call_target="tpu_custom_call" | custom-call | tf_op jit(solution)/shard_map/band/pallas_call | solution.py:499
  67.0 0.8 %deliver.1 = (bf16[288,384]{1,0:T(8,128)(2,1)}, bf16[288,384]{1,0:T(8,128)(2,1)}) custom-call(bf16[2,288,384]{2,1,0:T(8,128)(2,1)S(1)} %get-tuple-element.7.grads), custom_call_target="tpu_custom_call" | custom-call | tf_op jit(solution)/shard_map/deliver/pallas_call | solution.py:554

commit v5 on v4

--- a/solution.py
+++ b/solution.py
@@ -95,7 +95,7 @@
 
     class Link:
         def __init__(self, copy):
-            self.copy, self.waited = copy, False
+            self.copy, self.waited, self.sent = copy, False, False
 
         def start(self):
             self.copy.start()
@@ -117,11 +117,11 @@
         links.append(link)
         return link
 
-    def close():
-        for link in links:
-            if not link.waited:
-                link.copy.wait_recv()
-            link.copy.wait_send()
+    def settle(some):
+        for link in some:
+            if not link.sent:
+                link.sent = True
+                link.copy.wait_send()
 
     own_feat = [load(feats[w], fcols.at[w]) for w in (0, 1)]
     own_proj = [load(proj[w], projs.at[w, 0]) for w in (0, 1)]
@@ -179,7 +179,8 @@
     for p in (0, 1):
         for hh in (0, 1):
             target[1, p, hh * QUART:(hh + 1) * QUART] = sigmoid(steps_of(hh, 4 * p + 1) / 32.0)
-    gr[4 * HALF:] = jnp.zeros((HALF, EMB), F32)
+    for i in (0, 4):
+        gr[i * HALF:(i + 1) * HALF] = jnp.zeros((HALF, EMB), F32)
 
     def near_sum(w):
         to_sib[w].wait_recv()
@@ -282,14 +283,17 @@
             down[k].wait_recv()
 
     resp_sib[3], resp_sib[1] = resp_over(3), resp_over(1)
+    resp_two = []
     for k in pieces:
         pair[k].wait_recv()
-    resp_sib[2] = resp_over(2)
+        at = piece(2, c, k)
+        resp_two.append(remote(emb_r.at[at], emb_r.at[at], SIB))
     for k in pieces:
         p_near[k].wait_recv()
-        p_opp[k].wait_recv()
-    for i in (4, 3, 2, 1, 0):
-        resp_sib[i].wait_recv()
+    for link in [resp_sib[i] for i in (4, 3, 1, 0)] + resp_two:
+        link.wait_recv()
+
+    front = list(links)
 
     def push(i):
         grsib_s[i] = gr[quarter(i, 1 - c)].astype(BF)
@@ -332,8 +336,11 @@
         return pl.ds(pl.multiple_of((2 * p + kind * (1 - l)) * HALF, 64), ROWS)
 
     soon = 4 - pair_from
-    for p in (1, 0):
-        for kind in (0, 1):
+    for kind in (1, 0):
+        if kind == 0:
+            for link in p_opp:
+                link.wait_recv()
+        for p in (1, 0):
             slots = met(kind, p)
 
             def column(hh, s):
@@ -353,7 +360,7 @@
             coef = (scale * weight * (sig - goal)).astype(BF)
             coefs[kind, p] = coef
             term_r = dot(coef, emb_p[kind], TN)
-            if kind == 0:
+            if kind == 1:
                 gr[slots] = term_r
             else:
                 gr[slots] += term_r
@@ -395,28 +402,29 @@
     join(0, sib_zero)
     g_far, g_near = [], []
     for k in pieces:
-        home_pair[k].wait_recv()
-        add(pair_from, 2, k)
-
-        @pl.when(odd == 0)
-        def _():
-            fill(1, k)
-            home_down[k].start()
-
-        @pl.when(odd == 1)
-        def _():
-            fill(3, k)
-            home_up[k].start()
-
         g_opp[k].wait_recv()
         at = rows_at((1 - h) * QUART + k * PIECE, PIECE)
         gpsend[2, cut(k)] = (gp[1, at] + gprecv[0, cut(k)].astype(F32)).astype(BF)
         g_far.append(remote(gpsend.at[2, cut(k)], gprecv.at[2, cut(k)], FAR))
         g_near.append(remote(gpsend.at[1, cut(k)], gprecv.at[1, cut(k)], NEAR))
+        home_pair[k].wait_recv()
+        add(pair_from, 2, k)
+
+        @pl.when(odd == 0)
+        def _():
+            fill(1, k)
+            home_down[k].start()
+
+        @pl.when(odd == 1)
+        def _():
+            fill(3, k)
+            home_up[k].start()
 
     gather(gathered(0, 8), y, 4, y_peer)
-
-    d_far, d_sib, o_near, o_nearx = [[], []], [[], []], [None] * 2, [None] * 2
+    settle(front)
+    middle = [link for link in links if link not in home_z]
+
+    d_far, d_sib, o_near = [[], []], [[], []], [[], []]
 
     def back(w, k, g):
         u = unit[w, cut(k)]
@@ -424,12 +432,13 @@
         dsend[w, cut(k)] = ((g - u * inner) / norm[w, cut(k), 0:1]).astype(BF)
         d_far[w].append(remote(dsend.at[w, cut(k)], dbuf.at[w, piece(0, c, k)], FAR))
 
-    def product(w):
-        d = dsend[w]
-        osend[w, 0] = dot(d, projs[w, 0], NT).astype(BF)
-        osend[w, 1] = dot(d, projs[w, 1], NT).astype(BF)
-        o_near[w] = remote(osend.at[w, 0], onear.at[w, part(c)], NEAR)
-        o_nearx[w] = remote(osend.at[w, 1], onear.at[w, part(c)], NEARX)
+    def product(w, rows):
+        d = dsend[w, rows]
+        count = rows.stop - rows.start
+        for core, to in ((0, NEAR), (1, NEARX)):
+            osend[w, core, rows] = dot(d, projs[w, core], NT).astype(BF)
+            at = rows_at(c * QUART + rows.start, count)
+            o_near[w].append(remote(osend.at[w, core, rows], onear.at[w, at], to))
 
     def forward(w):
         for k in pieces:
@@ -449,12 +458,16 @@
         at = rows_at(h * QUART + k * PIECE, PIECE)
         back(1, k, gp[0, at] + gprecv[1, cut(k)].astype(F32) + gprecv[2, cut(k)].astype(F32))
     gather(gathered(1, 4), b // 8, 8, z_peer)
+    settle(middle)
     for k in pieces:
         home_z[k].wait_recv()
         back(0, k, gr[piece(0, c, k)] + grrecv[4, cut(k)].astype(F32))
-    product(1)
-    product(0)
-    forward(1)
+        if k == 0:
+            product(1, slice(0, QUART))
+        if k == 1:
+            product(0, slice(0, 2 * PIECE))
+            forward(1)
+    product(0, slice(2 * PIECE, QUART))
 
     def place(w, half, block):
         @pl.when(half == 0)
@@ -467,15 +480,16 @@
 
     for w in (1, 0):
         if w == 0:
+            settle(links)
             forward(0)
-        o_near[w].wait_recv()
-        o_nearx[w].wait_recv()
+        for link in o_near[w]:
+            link.wait_recv()
         place(w, h, onear[w].astype(F32).T.astype(BF))
         for link in d_sib[w]:
             link.wait_recv()
         place(w, 1 - h, dot(projs[w, 0], dbuf[w], NT).astype(BF))
     loss_ref[0] = jnp.sum(gathered(2, 8)) / (ROWS * BLOCKS * STEPS * ROWS)
-    close()
+    settle(links)
 
 
 def deliver(grads, out_r, out_p, sem):

time: 69.6 us -> 68.7 us (0.987)
  Pallas kernels: 65.8 us -> 64.9 us
    pallas_call x1, Pallas kernels: 65 us -> 64.1 us  [on_device(): pl.pallas_call(kernel, out_shape=(pltpu.VMEM((2, FEAT, ROWS), BF), jax.Sh...]
where the time goes in v5:
time: 68.7 us; the launch traced here: 68.6 us
  Pallas kernels  64.9 us (94%)
  between operations  3.7 us (5%)
    pallas_call x1, Pallas kernels, on_device(): pl.pallas_call(kernel, out_shape=(pltpu.VMEM((2, FEAT, ROWS), BF), jax.Sh...  64.1 us

profile of v5, /device:TPU:1, one launch (start us, length us, event | category | flops | bytes accessed | tf_op | source)
XLA Modules:
  0.0 68.6 jit_solution(7141637255160337269)
XLA Ops:
  1.9 64.1 %band.1 = (bf16[2,288,384]{2,1,0:T(8,128)(2,1)S(1)}, f32[1]{0:T(128)}) custom-call(bf16[288,384]{1,0:T(8,128)(2,1)} %bitcast.5, bf16[288,384]{1,0:T(8,128)(2,1)} %bitcast.6, bf16[288,1152]{1,0:T(8,128)(2,1)} %proj_r.1, bf16[288,1152]{1,0:T(8,128)(2,1)} %proj_p.1, f32[1]{0:T(128)S(6)} %copy.12.scale_ref, f32[1]{0:T(128)S(6)} %copy.13.bias_ref, ...), custom_call_target="tpu_custom_call" | custom-call | tf_op jit(solution)/shard_map/band/pallas_call | solution.py:513
  66.1 0.8 %deliver.1 = (bf16[288,384]{1,0:T(8,128)(2,1)}, bf16[288,384]{1,0:T(8,128)(2,1)}) custom-call(bf16[2,288,384]{2,1,0:T(8,128)(2,1)S(1)} %get-tuple-element.7.grads), custom_call_target="tpu_custom_call" | custom-call | tf_op jit(solution)/shard_map/deliver/pallas_call | solution.py:568

commit v6 on v5

--- a/solution.py
+++ b/solution.py
@@ -28,7 +28,7 @@
     fcols, frows, projs, part_sum, sib_send, sib_recv, feat_n, fsend, frecv, unit, norm, emb_p, emb_r,
     traw, tsend, trecv, target, vcols, vrows, coefs, gp, gr, gpsend, gprecv,
     grsib_s, grsib_r, grsend, grrecv, dsend, dbuf, osend, onear,
-    lmsg, lbuf, send_sem, recv_sem, loc_sem,
+    losses, lmsg, lbuf, send_sem, recv_sem, loc_sem,
 ):
     b = lax.axis_index("batch")
     t = lax.axis_index("tower")
@@ -290,7 +290,7 @@
         resp_two.append(remote(emb_r.at[at], emb_r.at[at], SIB))
     for k in pieces:
         p_near[k].wait_recv()
-    for link in [resp_sib[i] for i in (4, 3, 1, 0)] + resp_two:
+    for link in [resp_sib[i] for i in (4, 3, 1, 0)]:
         link.wait_recv()
 
     front = list(links)
@@ -330,40 +330,54 @@
                 home_down[k].start()
 
     scale, bias = scale_ref[0], bias_ref[0]
-    loss = jnp.zeros((8, ROWS), F32)
+    losses[...] = jnp.zeros((8, ROWS), F32)
 
     def met(kind, p):
         return pl.ds(pl.multiple_of((2 * p + kind * (1 - l)) * HALF, 64), ROWS)
 
     soon = 4 - pair_from
-    for kind in (1, 0):
-        if kind == 0:
-            for link in p_opp:
-                link.wait_recv()
-        for p in (1, 0):
-            slots = met(kind, p)
-
-            def column(hh, s):
-                at = 4 * p + s
-                return vrows[kind, quarter(hh, c), at:at + 1]
-
-            weight = jnp.concatenate(
-                [jnp.where(early, column(hh, kind), column(hh, kind + 2)) for hh in (0, 1)], axis=0
-            )
-            goal = target[kind, p]
-            z = scale * dot(emb_p[kind], emb_r[slots], NT) + bias
-            e = jnp.exp(-jnp.abs(z))
-            soft = jnp.maximum(z, 0.0) + jnp.log1p(e)
-            sig = jnp.where(z >= 0, 1.0, e) / (1.0 + e)
-            cost = weight * (soft - goal * z)
-            loss = loss + jnp.sum(cost.reshape(HALF // 8, 8, ROWS), axis=0)
-            coef = (scale * weight * (sig - goal)).astype(BF)
-            coefs[kind, p] = coef
-            term_r = dot(coef, emb_p[kind], TN)
-            if kind == 1:
-                gr[slots] = term_r
-            else:
-                gr[slots] += term_r
+    def tile(kind, p):
+        slots = met(kind, p)
+
+        def column(hh, s):
+            at = 4 * p + s
+            return vrows[kind, quarter(hh, c), at:at + 1]
+
+        weight = jnp.concatenate(
+            [jnp.where(early, column(hh, kind), column(hh, kind + 2)) for hh in (0, 1)], axis=0
+        )
+        goal = target[kind, p]
+        z = scale * dot(emb_p[kind], emb_r[slots], NT) + bias
+        e = jnp.exp(-jnp.abs(z))
+        soft = jnp.maximum(z, 0.0) + jnp.log1p(e)
+        sig = jnp.where(z >= 0, 1.0, e) / (1.0 + e)
+        cost = weight * (soft - goal * z)
+        losses[...] += jnp.sum(cost.reshape(HALF // 8, 8, ROWS), axis=0)
+        coef = (scale * weight * (sig - goal)).astype(BF)
+        coefs[kind, p] = coef
+        term_r = dot(coef, emb_p[kind], TN)
+        if kind == 1:
+            gr[slots] = term_r
+        else:
+            gr[slots] += term_r
+
+    for early_l in (0, 1):
+        @pl.when(l == early_l)
+        def _():
+            tile(1, 1 - early_l)
+
+    for link in resp_two:
+        link.wait_recv()
+    for early_l in (0, 1):
+        @pl.when(l == early_l)
+        def _():
+            tile(1, early_l)
+
+    for link in p_opp:
+        link.wait_recv()
+    tile(0, 1)
+    tile(0, 0)
+    loss = losses[...]
 
     gathers = []
 
@@ -551,6 +565,7 @@
             vm(2, HALF, EMB),
             vm(2, 2, QUART, FEAT),
             vm(2, HALF, FEAT),
+            vm(8, ROWS, kind=F32),
             vm(3, 8, 128, kind=F32),
             vm(3, 8, 8, 128, kind=F32),
             pltpu.SemaphoreType.DMA((128,)),

time: 68.7 us -> 68.1 us (level)
  no operation moved by 1% of the time
where the time goes in v6:
time: 68.1 us; the launch traced here: 68 us
  Pallas kernels  64.3 us (94%)
  between operations  3.7 us (5%)
    pallas_call x1, Pallas kernels, on_device(): pl.pallas_call(kernel, out_shape=(pltpu.VMEM((2, FEAT, ROWS), BF), jax.Sh...  63.5 us

profile of v6, /device:TPU:1, one launch (start us, length us, event | category | flops | bytes accessed | tf_op | source)
XLA Modules:
  0.0 68.0 jit_solution(17089042848951100513)
XLA Ops:
  1.9 63.5 %band.1 = (bf16[2,288,384]{2,1,0:T(8,128)(2,1)S(1)}, f32[1]{0:T(128)}) custom-call(bf16[288,384]{1,0:T(8,128)(2,1)} %bitcast.5, bf16[288,384]{1,0:T(8,128)(2,1)} %bitcast.6, bf16[288,1152]{1,0:T(8,128)(2,1)} %proj_r.1, bf16[288,1152]{1,0:T(8,128)(2,1)} %proj_p.1, f32[1]{0:T(128)S(6)} %copy.12.scale_ref, f32[1]{0:T(128)S(6)} %copy.13.bias_ref, ...), custom_call_target="tpu_custom_call" | custom-call | tf_op jit(solution)/shard_map/band/pallas_call | solution.py:527
  65.5 0.8 %deliver.1 = (bf16[288,384]{1,0:T(8,128)(2,1)}, bf16[288,384]{1,0:T(8,128)(2,1)}) custom-call(bf16[2,288,384]{2,1,0:T(8,128)(2,1)S(1)} %get-tuple-element.7.grads), custom_call_target="tpu_custom_call" | custom-call | tf_op jit(solution)/shard_map/deliver/pallas_call | solution.py:583

commit v7 on v6

--- a/solution.py
+++ b/solution.py
@@ -133,11 +133,12 @@
         part_sum[w] = dot(frows[w, rows_at((1 - h) * HALF, HALF)], projs[w, 0])
         sib_send[w] = part_sum[w, part(1 - c)].astype(BF)
 
-    for w in (0, 1):
+    def turn(w):
         own_feat[w].wait()
         frows[w] = fcols[w].astype(F32).T.astype(BF)
-        if w == 0:
-            own_sum(0)
+
+    turn(0)
+    own_sum(0)
     pl.semaphore_wait(barrier, len(peers))
 
     sum_sib, to_sib, feat_near, feat_nearx, partial = [], [], [], [], []
@@ -148,6 +149,7 @@
         feat_nearx.append(remote(frows.at[w, quarter(h, 1 - c)], feat_n.at[w, 1], NEARX))
 
     enter(0)
+    turn(1)
     own_sum(1)
     enter(1)
     pieces = range(QUART // PIECE)

time: 68.1 us -> 68.1 us (level)
  no operation moved by 1% of the time
where the time goes in v7:
time: 68.1 us; the launch traced here: 68 us
  Pallas kernels  64.3 us (94%)
  between operations  3.7 us (5%)
    pallas_call x1, Pallas kernels, on_device(): pl.pallas_call(kernel, out_shape=(pltpu.VMEM((2, FEAT, ROWS), BF), jax.Sh...  63.5 us

profile of v7, /device:TPU:1, one launch (start us, length us, event | category | flops | bytes accessed | tf_op | source)
XLA Modules:
  0.0 68.0 jit_solution(15582437502699842060)
XLA Ops:
  1.9 63.5 %band.1 = (bf16[2,288,384]{2,1,0:T(8,128)(2,1)S(1)}, f32[1]{0:T(128)}) custom-call(bf16[288,384]{1,0:T(8,128)(2,1)} %bitcast.5, bf16[288,384]{1,0:T(8,128)(2,1)} %bitcast.6, bf16[288,1152]{1,0:T(8,128)(2,1)} %proj_r.1, bf16[288,1152]{1,0:T(8,128)(2,1)} %proj_p.1, f32[1]{0:T(128)S(6)} %copy.12.scale_ref, f32[1]{0:T(128)S(6)} %copy.13.bias_ref, ...), custom_call_target="tpu_custom_call" | custom-call | tf_op jit(solution)/shard_map/band/pallas_call | solution.py:529
  65.4 0.8 %deliver.1 = (bf16[288,384]{1,0:T(8,128)(2,1)}, bf16[288,384]{1,0:T(8,128)(2,1)}) custom-call(bf16[2,288,384]{2,1,0:T(8,128)(2,1)S(1)} %get-tuple-element.7.grads), custom_call_target="tpu_custom_call" | custom-call | tf_op jit(solution)/shard_map/deliver/pallas_call | solution.py:585
